TPU v7x, 512 devices: a whole 4x8x8 slice. The times are simulated.
512 devices in a mesh: vocab: 8 (over y), row: 8 (over z_hi, core), width: 8 (over z_lo, x).
Axes of the slice: x: 4, y: 8, z: 8 (z_hi: 4, z_lo: 2; z = z_hi * 2 + z_lo), core: 2. Of those that a mesh axis runs over, the one named last changes fastest.
Arguments:
- hidden: bfloat16 [768, 8192], P(None, 'width'), may hold values from -1500 to 1500
- unembed: bfloat16 [8, 4008, 8192], P('vocab', 'row', 'width'), may hold values from -0.06591797 to 0.06591797
- rotate_vocab: bfloat16 [8, 4008, 4008], P('vocab', 'width', 'row'), may hold values from -0.8515625 to 0.8515625
- rotate_width: bfloat16 [8192, 4096], P('width', 'row'), may hold values from -0.0625 to 0.0625
- labels: int32 [768], replicated, may hold values from 0 to 128255
- seq_ids: int32 [768], replicated, may hold values from 0 to 11, never falling along the last dimension, each value on 1 to 128 neighbouring positions
Outputs:
- eigenvalues: float32 [8, 4008, 4096], P('vocab', 'width', 'row')
Inputs may be any that keep to these rules, and one draw needn't show every extreme that they name: seq_ids never falls along the tokens; every sequence holds 1 to 128 tokens, one exactly 128.
All inputs are finite; a program needn't handle non-finite values.
Results may differ from a plain program's by a relative error of at most 0.0048.
Values may be sent and summed in bfloat16 or wider, within the bound.
No kernel may reach another device: no remote copies, remote signals or barrier semaphores. Data moves between devices by JAX's collectives and lax.ppermute only.
A program may use at most 64 MiB of HBM per device.

v0:
```python
import jax
import jax.numpy as jnp
from jax import lax
from jax.sharding import PartitionSpec as P

SEQ_LEN = 128
SEQS = 12


def window_rows(values, starts, span):

    def one_window(begin):
        return lax.dynamic_slice_in_dim(values, begin, span, 0)

    return jax.vmap(one_window)(starts)


def body(hidden, unembed, rotate_vocab, rotate_width, labels, seq_ids):
    tokens = hidden.shape[0]
    local_rows = unembed.shape[1]
    block_rows = unembed[0]
    partial_value = lax.dot_general(
        hidden, block_rows, (((1,), (1,)), ((), ())), preferred_element_type=jnp.float32
    )
    logits = lax.psum(partial_value, "width")
    local_top = jnp.max(logits, axis=1)
    largest = lax.pmax(local_top, ("vocab", "row"))
    scaled = jnp.exp(logits - largest[:, None])
    summed = lax.psum(jnp.sum(scaled, axis=1), ("vocab", "row"))
    probabilities = scaled / summed[:, None]
    first_row = (
        lax.axis_index("vocab") * lax.axis_size("row") + lax.axis_index("row")
    ) * local_rows
    window_index = first_row + jnp.arange(local_rows, dtype=jnp.int32)
    onehot = (labels[:, None] == window_index[None, :]).astype(jnp.float32)
    errors = (probabilities - onehot).astype(jnp.bfloat16)
    eigen_basis = rotate_vocab[0]
    partial_turn = lax.dot_general(
        errors, eigen_basis, (((1,), (1,)), ((), ())), preferred_element_type=jnp.float32
    )
    turned = lax.psum(partial_turn, "row").astype(jnp.bfloat16)
    partial_projection = jnp.dot(hidden, rotate_width, preferred_element_type=jnp.float32)
    projected = lax.psum(partial_projection, "width").astype(jnp.bfloat16)
    sequence_index = jnp.arange(SEQS, dtype=jnp.int32)
    before = (seq_ids[None, :] < sequence_index[:, None]).astype(jnp.int32)
    starts = jnp.minimum(jnp.sum(before, axis=1), tokens - SEQ_LEN)
    member = window_rows(seq_ids, starts, SEQ_LEN) == sequence_index[:, None]
    turned_windows = jnp.where(
        member[:, :, None], window_rows(turned, starts, SEQ_LEN), jnp.zeros((), jnp.bfloat16)
    )
    projected_windows = window_rows(projected, starts, SEQ_LEN)
    gradients = jnp.einsum(
        "sta,stj->saj", turned_windows, projected_windows, preferred_element_type=jnp.float32
    )
    return jnp.sum(gradients * gradients, axis=0)[None]


def solution(mesh):
    in_specs = (
        P(None, "width"),
        P("vocab", "row", "width"),
        P("vocab", "width", "row"),
        P("width", "row"),
        P(),
        P(),
    )
    out_specs = P("vocab", "width", "row")
    return jax.shard_map(body, mesh=mesh, in_specs=in_specs, out_specs=out_specs, check_vma=False)
```

profile of v0, /device:TPU:1, one launch (start us, length us, event | category | flops | bytes accessed | tf_op | source)
XLA Modules:
  0.0 512.6 jit_solution(11977498214839711881)
XLA Ops:
  6.5 1.4 copy-done
  7.9 3.4 fusion.3
  12.6 2.1 fusion.9
  14.7 66.6 %all-reduce.7 = bf16[768,512]{1,0:T(8,128)(2,1)S(1)} all-reduce(f32[768,512]{1,0:T(8,128)} %fusion.9), channel_id=1, replica_groups=mesh['vocab'=8,'row'=8,'width'=8] {'width'}, use_global_device_ids=true, to_apply=%region_7.0 | all-reduce | flops 393216 | bytes 2359296 | tf_op jit(solution)/shard_map/psum | solution.py:43
  81.3 14.4 %while.6 = (s32[]{:T(128)}, s32[768]{0:T(1024)S(1)}, s32[12,1]{0,1:T(1,128)S(1)}, s32[12,128]{1,0:T(8,128)S(1)}) while((s32[]{:T(128)}, s32[768]{0:T(1024)S(1)}, s32[12,1]{0,1:T(1,128)S(1)}, s32[12,128]{1,0:T(8,128)S(1)}) %tuple.59), condition=%wide.while_cond.clone, body=%wide.while_body.sunk.clone | while | flops 2 | bytes 2121 | solution.py:13
  81.9 0.6 dynamic-slice_bitcast_fusion.3
  83.1 0.6 dynamic-slice_bitcast_fusion.3
  84.2 0.6 dynamic-slice_bitcast_fusion.3
  85.4 0.6 dynamic-slice_bitcast_fusion.3
  86.6 0.6 dynamic-slice_bitcast_fusion.3
  87.8 0.6 dynamic-slice_bitcast_fusion.3
  89.0 0.6 dynamic-slice_bitcast_fusion.3
  90.2 0.6 dynamic-slice_bitcast_fusion.3
  91.4 0.6 dynamic-slice_bitcast_fusion.3
  92.6 0.6 dynamic-slice_bitcast_fusion.3
  95.7 21.4 %while.8 = (s32[]{:T(128)}, bf16[768,512]{1,0:T(8,128)(2,1)S(1)}, s32[12,2]{0,1:T(2,128)S(1)}, bf16[12,128,512]{2,1,0:T(8,128)(2,1)}) while((s32[]{:T(128)}, bf16[768,512]{1,0:T(8,128)(2,1)S(1)}, s32[12,2]{0,1:T(2,128)S(1)}, bf16[12,128,512]{2,1,0:T(8,128)(2,1)}) %tuple.47), condition=%wide.while_cond.2.clone, body=%wide.while_body.2.sunk.clone | while | flops 2 | bytes 263249 | solution.py:13
  96.2 1.2 bitcast_dynamic-update-slice_fusion.7
  98.0 1.2 bitcast_dynamic-update-slice_fusion.7
  99.8 1.2 bitcast_dynamic-update-slice_fusion.7
  101.6 1.2 bitcast_dynamic-update-slice_fusion.7
  103.4 1.2 bitcast_dynamic-update-slice_fusion.7
  105.1 1.2 bitcast_dynamic-update-slice_fusion.7
  106.9 1.2 bitcast_dynamic-update-slice_fusion.7
  108.7 1.2 bitcast_dynamic-update-slice_fusion.7
  110.5 1.2 bitcast_dynamic-update-slice_fusion.7
  112.3 1.2 bitcast_dynamic-update-slice_fusion.7
  114.1 1.2 bitcast_dynamic-update-slice_fusion.7
  115.8 1.2 bitcast_dynamic-update-slice_fusion.7
  117.1 1.6 reduce_max.9
  118.7 157.5 %pmax.7 = f32[768]{0:T(1024)S(1)} all-reduce(f32[768]{0:T(1024)S(1)} %reduce_max.9), channel_id=1, replica_groups=mesh['vocab'=8,'row'=8,'width'=8] {'vocab','row'}, use_global_device_ids=true, to_apply=%region_3.0 | all-reduce | flops 768 | bytes 6144 | tf_op jit(solution)/shard_map/pmax | solution.py:27
  276.5 138.0 %psum.29 = f32[768]{0:T(1024)S(1)} all-reduce(f32[768]{0:T(1024)S(1)} %fusion.2), channel_id=1, replica_groups=mesh['vocab'=8,'row'=8,'width'=8] {'vocab','row'}, use_global_device_ids=true, to_apply=%region_5.0 | all-reduce | flops 768 | bytes 6144 | tf_op jit(solution)/shard_map/psum | solution.py:29
  414.5 3.1 fusion.6
  417.6 59.2 %all-reduce.6 = bf16[768,501]{1,0:T(8,128)(2,1)S(1)} all-reduce(f32[768,501]{1,0:T(8,128)} %fusion.6), channel_id=1, replica_groups=mesh['vocab'=8,'row'=8,'width'=8] {'row'}, use_global_device_ids=true, to_apply=%region_6.0 | all-reduce | flops 384768 | bytes 2308608 | tf_op jit(solution)/shard_map/psum | solution.py:41
  476.7 23.0 %while.7 = (s32[]{:T(128)}, bf16[768,501]{1,0:T(8,128)(2,1)S(1)}, s32[12,2]{0,1:T(2,128)S(1)}, bf16[12,128,501]{2,1,0:T(8,128)(2,1)}) while((s32[]{:T(128)}, bf16[768,501]{1,0:T(8,128)(2,1)S(1)}, s32[12,2]{0,1:T(2,128)S(1)}, bf16[12,128,501]{2,1,0:T(8,128)(2,1)}) %tuple.58), condition=%wide.while_cond.1.clone, body=%wide.while_body.1.sunk.clone | while | flops 2 | bytes 260433 | solution.py:13
  477.3 1.3 bitcast_dynamic-update-slice_fusion.6
  479.2 1.3 bitcast_dynamic-update-slice_fusion.6
  481.2 1.3 bitcast_dynamic-update-slice_fusion.6
  483.1 1.3 bitcast_dynamic-update-slice_fusion.6
  485.0 1.3 bitcast_dynamic-update-slice_fusion.6
  486.9 1.3 bitcast_dynamic-update-slice_fusion.6
  488.8 1.3 bitcast_dynamic-update-slice_fusion.6
  490.7 1.3 bitcast_dynamic-update-slice_fusion.6
  492.7 1.3 bitcast_dynamic-update-slice_fusion.6
  494.6 1.3 bitcast_dynamic-update-slice_fusion.6
  496.5 1.3 bitcast_dynamic-update-slice_fusion.6
  498.4 1.3 bitcast_dynamic-update-slice_fusion.6
  499.8 4.3 multiply_reduce_fusion
  504.1 1.7 broadcast_in_dim.12
  (95 shorter events, 23.3 us)
Async XLA Ops:
  6.5 1.4 copy-start
  6.5 110.5 %all-reduce.5.cloned.1.call-start = ((), (), s32[]{:S(2)}) async-start(), calls=%async_computation | async-start | bytes 3096576 | tf_op jit(solution)/shard_map/psum | solution.py:25
  11.3 0.7 copy-start.2
  11.3 1.2 copy-start.3
  117.1 297.4 %copy-start.4 = (s32[768]{0:T(1024)S(1)}, s32[768]{0:T(1024)}, u32[]{:S(2)}) copy-start(s32[768]{0:T(1024)} %param.10) | copy-start | bytes 9220
  117.1 159.2 %copy-start.1 = (f32[768,501]{0,1:T(8,128)S(1)}, f32[768,501]{0,1:T(8,128)}, u32[]{:S(2)}) copy-start(f32[768,501]{0,1:T(8,128)} %all-reduce.5.cloned.1.call-done) | copy-start | bytes 4617220
Sparse Core Ops, SparseCore 0:
  11.5 96.1 all-reduce.4
where the time goes:
time: 517 us; the launch traced here: 513 us
  blocking collectives  421 us (81%)
  local copies, waits for them, and re-layouts  62.8 us (12%)
  between operations  13.5 us (3%)
  matrix products  12.9 us (2%)
    pmax x1, blocking collectives, body(): largest = lax.pmax(local_top, ('vocab', 'row'))  158 us
    psum x1, blocking collectives, body(): summed = lax.psum(jnp.sum(scaled, axis=1), ('vocab', 'row'))  138 us
    psum x1, blocking collectives, body(): projected = lax.psum(partial_projection, 'width').astype(jnp.bfloat16)  66.6 us
    psum x1, blocking collectives, body(): turned = lax.psum(partial_turn, 'row').astype(jnp.bfloat16)  59.2 us
    gather x108, local copies, waits for them, and re-layouts  58.7 us
  transfers between devices with their start and end apart: 1, of which 0 were waited for; matrix products, arithmetic and copies ran while one was open for 7% of the time, Pallas kernels for 0%

commit v1 on v0

v1 whole, which is shorter than its diff:
```python
import functools

import jax
import jax.numpy as jnp
from jax import lax
from jax.experimental import pallas as pl
from jax.experimental.pallas import tpu as pltpu
from jax.sharding import Mesh
from jax.sharding import PartitionSpec as P

SEQ_LEN = 128
SEQS = 12
PARTS = 8
CORES = 2
CHIPS = PARTS // CORES
TOKENS = 768
GROUP = TOKENS // PARTS
BLOCK = GROUP // CORES
DEALT = BLOCK // PARTS
SHARE = 8
ROWS = BLOCK + SHARE
LANES = 512
WINDOW = SEQ_LEN + 16
VMEM = 48 * 1024 * 1024
MOST = 60 * 1024 * 1024

FULL = pl.BlockSpec(memory_space=pltpu.VMEM)
SCALARS = pl.BlockSpec(memory_space=pltpu.SMEM)
ROW = ("chip", "core")


def call(kernel, outs, ins):
    shapes = [jax.ShapeDtypeStruct(s, d) for s, d in outs]
    return pl.pallas_call(
        kernel,
        out_shape=shapes if len(shapes) > 1 else shapes[0],
        in_specs=ins,
        out_specs=[FULL] * len(shapes) if len(shapes) > 1 else FULL,
        compiler_params=pltpu.CompilerParams(vmem_limit_bytes=VMEM),
    )


def pick(shape, source):
    row = lax.broadcasted_iota(jnp.int32, shape, 0)
    column = lax.broadcasted_iota(jnp.int32, shape, 1)
    return (column == source(row)).astype(jnp.float32).astype(jnp.bfloat16)


def partial_kernel(place_ref, hidden_ref, mine_ref, unembed_ref, width_ref, out_ref):
    rows = unembed_ref.shape[1]
    cores, each = out_ref.shape[:2]
    logits = lax.dot_general(
        hidden_ref[...], unembed_ref[0], (((1,), (1,)), ((), ())), preferred_element_type=jnp.float32
    )
    first = pl.program_id(0) * each

    def source(row):
        piece, within = row // SHARE, lax.rem(row, SHARE)
        owner = (first + lax.rem(piece, each)) * cores + piece // each
        return jnp.where(within < DEALT, owner * DEALT + within, -1)

    dealt = jnp.dot(pick((cores * each * SHARE, GROUP), source), mine_ref[...], preferred_element_type=jnp.float32)
    projected = jnp.dot(dealt.astype(jnp.bfloat16), width_ref[...], preferred_element_type=jnp.float32)
    for core in range(cores):
        for width in range(each):
            piece = core * each + width
            out_ref[core, width, :BLOCK, rows:] = jnp.zeros((BLOCK, LANES - rows), jnp.float32)
            out_ref[core, width, :BLOCK, :rows] = logits[piece * BLOCK : (piece + 1) * BLOCK]
            out_ref[core, width, BLOCK:, :] = projected[piece * SHARE : (piece + 1) * SHARE]


def partial_sums(place, hidden, unembed, rotate_width):
    each = PARTS // CHIPS
    features, columns = rotate_width.shape
    rows = unembed.shape[1]
    return pl.pallas_call(
        partial_kernel,
        out_shape=jax.ShapeDtypeStruct((CORES, PARTS, ROWS, LANES), jnp.float32),
        grid_spec=pltpu.PrefetchScalarGridSpec(
            num_scalar_prefetch=1,
            grid=(CHIPS,),
            in_specs=[
                pl.BlockSpec((CORES * GROUP, features), lambda g, place: (g, 0)),
                pl.BlockSpec((GROUP, features), lambda g, place: (place[0], 0)),
                pl.BlockSpec((1, rows, features), lambda g, place: (0, 0, 0)),
                pl.BlockSpec((features, columns), lambda g, place: (0, 0)),
            ],
            out_specs=pl.BlockSpec((CORES, each, ROWS, LANES), lambda g, place: (0, g, 0, 0)),
        ),
        compiler_params=pltpu.CompilerParams(vmem_limit_bytes=MOST),
    )(place, hidden, hidden, unembed, rotate_width)


def local_kernel(rows, core_ref, pieces_ref, logits_ref, stats_ref, keep_ref, send_ref):
    sums = [jnp.sum(pieces_ref[core * PARTS : (core + 1) * PARTS], axis=0) for core in range(CORES)]
    column = lax.broadcasted_iota(jnp.int32, (CORES * BLOCK, LANES), 1)
    logits = jnp.concatenate([part[:BLOCK] for part in sums], axis=0)
    logits = jnp.where(column < rows, logits, -jnp.inf)
    logits_ref[...] = logits
    first = core_ref[0] == 0
    keep_ref[...] = jnp.where(first, sums[0][BLOCK:], sums[1][BLOCK:])
    send_ref[...] = jnp.where(first, sums[1][BLOCK:], sums[0][BLOCK:])
    largest = jnp.max(logits, axis=1, keepdims=True)
    largest = jnp.maximum(largest[:BLOCK], largest[BLOCK:])
    total = jnp.sum(jnp.exp(logits - jnp.concatenate([largest, largest], axis=0)), axis=1, keepdims=True)
    total = total[:BLOCK] + total[BLOCK:]
    lane = lax.broadcasted_iota(jnp.int32, (BLOCK, 128), 1)
    square = jnp.concatenate(
        [jnp.where(lane == 0, largest, total), jnp.zeros((128 - BLOCK, 128), jnp.float32)], axis=0
    )
    tile = square.T[: stats_ref.shape[1]]
    for device in range(stats_ref.shape[0]):
        stats_ref[device] = tile


def error_kernel(rows, place_ref, logits_ref, stats_ref, labels_ref, keep_ref, got_ref, out_ref):
    largest = jnp.max(stats_ref[:, 0:1, :], axis=0)
    total = jnp.sum(stats_ref[:, 1:2, :] * jnp.exp(stats_ref[:, 0:1, :] - largest[None]), axis=0)
    row = lax.broadcasted_iota(jnp.int32, (128, 128), 0)
    square = jnp.where(row == 0, largest, total).T
    largest, total = square[:BLOCK, 0:1], square[:BLOCK, 1:2]
    column = lax.broadcasted_iota(jnp.int32, (BLOCK, LANES), 1)
    parts = []
    for core in range(CORES):
        probabilities = jnp.exp(logits_ref[core * BLOCK : (core + 1) * BLOCK] - largest) / total
        hit = (labels_ref[...] - (place_ref[1] + core * rows) == column) & (column < rows)
        parts.append((probabilities - hit.astype(jnp.float32)).astype(jnp.bfloat16))
    errors = jnp.concatenate(parts, axis=0)
    first = place_ref[0] == 0
    keep, got = keep_ref[...], got_ref[...]
    share = jnp.concatenate([jnp.where(first, keep, got), jnp.where(first, got, keep)], axis=0).astype(jnp.bfloat16)
    for piece in range(PARTS):
        out_ref[piece, : CORES * BLOCK] = errors
        out_ref[piece, CORES * BLOCK :] = share


def turn_kernel(core_ref, packed_ref, basis_ref, other_ref, out_ref, share_ref):
    rows = basis_ref.shape[1]
    turned = 0.0
    for core, ref in ((core_ref[0], basis_ref), (1 - core_ref[0], other_ref)):
        errors = packed_ref[:, pl.ds(pl.multiple_of(core * BLOCK, BLOCK), BLOCK), :].reshape(PARTS * BLOCK, LANES)
        turned += lax.dot_general(
            errors[:, :rows], ref[0], (((1,), (1,)), ((), ())), preferred_element_type=jnp.float32
        )
    out_ref[:, :, :rows] = turned.astype(jnp.bfloat16).reshape(CHIPS, GROUP, rows)
    out_ref[:, :, rows:] = jnp.zeros((CHIPS, GROUP, LANES - rows), jnp.bfloat16)
    dealt = packed_ref[:, CORES * BLOCK :, :].reshape(PARTS * CORES * SHARE, LANES)
    order = pick((GROUP, PARTS * CORES * SHARE), lambda row: row // DEALT * SHARE + lax.rem(row, DEALT))
    share = jnp.dot(order, dealt, preferred_element_type=jnp.float32).astype(jnp.bfloat16)
    for piece in range(PARTS):
        share_ref[piece] = share


def sum_kernel(pieces_ref, out_ref):
    out_ref[...] = jnp.sum(pieces_ref[...].astype(jnp.float32), axis=0).astype(jnp.bfloat16)


def gradient_kernel(starts_ref, turned_ref, projected_ref, out_ref, total_ref):
    for sequence in range(SEQS):
        start, end = starts_ref[sequence], starts_ref[sequence + 1]
        begin = pl.multiple_of(jnp.minimum(start // 16 * 16, TOKENS - WINDOW), 16)
        token = begin + lax.broadcasted_iota(jnp.int32, (WINDOW, 1), 0)
        member = (token >= start) & (token < end)
        turned = turned_ref[pl.ds(begin, WINDOW), :]
        turned = jnp.where(member, turned, jnp.zeros((), jnp.bfloat16))
        gradient = lax.dot_general(
            turned,
            projected_ref[pl.ds(begin, WINDOW), :],
            (((0,), (0,)), ((), ())),
            preferred_element_type=jnp.float32,
        )
        if sequence == 0:
            total_ref[...] = gradient * gradient
        elif sequence < SEQS - 1:
            total_ref[...] += gradient * gradient
        else:
            total = total_ref[...] + gradient * gradient
            tile, width = total.shape
            pieces = width // 128
            for piece in range(pieces):
                out_ref[pl.ds(piece, tile, stride=pieces), :] = total[:, piece * 128 : (piece + 1) * 128]


def gradients(starts, turned, projected, height):
    width = projected.shape[1]
    tile, pieces = 128, width // 128
    flat = pl.pallas_call(
        gradient_kernel,
        out_shape=jax.ShapeDtypeStruct((height * pieces, 128), jnp.float32),
        grid_spec=pltpu.PrefetchScalarGridSpec(
            num_scalar_prefetch=1,
            grid=(LANES // tile,),
            in_specs=[
                pl.BlockSpec((TOKENS, tile), lambda g, starts: (0, g)),
                pl.BlockSpec((TOKENS, width), lambda g, starts: (0, 0)),
            ],
            out_specs=pl.BlockSpec((tile * pieces, 128), lambda g, starts: (g, 0)),
            scratch_shapes=[pltpu.VMEM((tile, width), jnp.float32)],
        ),
        compiler_params=pltpu.CompilerParams(vmem_limit_bytes=VMEM),
    )(starts, turned, projected)
    return flat.reshape(1, height, width)


def exchange(values, axis):
    return lax.all_to_all(values, axis, 0, 0, tiled=True)


def swap(values):
    return lax.ppermute(values, "core", [(i, CORES - 1 - i) for i in range(CORES)])


def body(hidden, unembed, rotate_vocab, rotate_width, labels, seq_ids):
    rows = unembed.shape[1]
    vocab, chip, core, width = (lax.axis_index(a).astype(jnp.int32) for a in ("vocab", "chip", "core", "width"))
    place = jnp.stack([core, (vocab * PARTS + chip * CORES) * rows])
    core = core.reshape(1)
    owned = (width // CORES * CORES + core[0]) * GROUP + lax.rem(width, CORES) * BLOCK
    mine = lax.dynamic_slice_in_dim(labels, owned, BLOCK, 0).reshape(BLOCK, 1)
    sequence_index = jnp.arange(SEQS + 1, dtype=jnp.int32)
    starts = jnp.sum((seq_ids[None, :] < sequence_index[:, None]).astype(jnp.int32), axis=1)
    half, single = jnp.bfloat16, jnp.float32

    pieces = partial_sums(vocab.reshape(1), hidden, unembed, rotate_width)
    pieces = exchange(pieces.reshape(CORES * PARTS, ROWS, LANES), ("core", "width"))
    logits, stats, keep, send = call(
        functools.partial(local_kernel, rows),
        [
            ((CORES * BLOCK, LANES), single),
            ((PARTS * CHIPS, 2, 128), single),
            ((SHARE, LANES), single),
            ((SHARE, LANES), single),
        ],
        [SCALARS, FULL],
    )(core, pieces)
    stats = exchange(stats, ("vocab", "chip"))
    packed = call(
        functools.partial(error_kernel, rows),
        [((PARTS, CORES * ROWS, LANES), half)],
        [SCALARS, FULL, FULL, FULL, FULL, FULL],
    )(place, logits, stats, mine, keep, swap(send))
    turned, share = call(
        turn_kernel,
        [((CHIPS, GROUP, LANES), half), ((PARTS, GROUP, LANES), half)],
        [SCALARS, FULL, FULL, FULL],
    )(core, exchange(packed, "width"), rotate_vocab, swap(rotate_vocab))
    projected = exchange(share, "vocab").reshape(TOKENS, LANES)
    turned = call(sum_kernel, [((GROUP, LANES), half)], [FULL])(exchange(turned, "chip"))
    turned = lax.all_gather(turned, ROW, axis=0, tiled=True)
    return gradients(starts, turned, projected, rows)


def solution(mesh):
    vocab, row, width = mesh.axis_names
    devices = mesh.devices.reshape(PARTS, CHIPS, CORES, PARTS)
    in_specs = (
        P(None, width),
        P(vocab, ROW, width),
        P(vocab, width, ROW),
        P(width, ROW),
        P(),
        P(),
    )
    return jax.shard_map(
        body,
        mesh=Mesh(devices, (vocab, *ROW, width)),
        in_specs=in_specs,
        out_specs=P(vocab, width, ROW),
        check_vma=False,
    )
```

time: 517 us -> 132 us (0.26)
  the two profiles are of different devices: /device:TPU:1 before, /device:TPU:67 now
where the time goes in v1:
time: 132 us
  waiting for transfers between devices  44 us (33%)
  starting transfers between devices  37.6 us (28%)
  blocking collectives  33.5 us (25%)
  Pallas kernels  14.3 us (11%)
  local copies, waits for them, and re-layouts  2.15 us (2%)
    all_to_all x4, waiting for transfers between devices, exchange(): return lax.all_to_all(values, axis, 0, 0, tiled=True)  41.8 us
    all_to_all x4, starting transfers between devices, exchange(): return lax.all_to_all(values, axis, 0, 0, tiled=True)  29.9 us
    all_gather x1, blocking collectives, body(): turned = lax.all_gather(turned, ROW, axis=0, tiled=True)  18.2 us
    all_to_all x1, blocking collectives, exchange(): return lax.all_to_all(values, axis, 0, 0, tiled=True)  15.3 us
    ppermute x2, starting transfers between devices, swap(): lax.ppermute(values, 'core', [(i, CORES - 1 - i) for i in range(CORES)])  7.63 us
    pallas_call x1, Pallas kernels, partial_sums(): pl.pallas_call(partial_kernel, out_shape=jax.ShapeDtypeStruct((CORES, PAR...  6.05 us
    pallas_call x1, Pallas kernels, gradients(): pl.pallas_call(gradient_kernel, out_shape=jax.ShapeDtypeStruct((height *...  3.95 us
  transfers between devices with their start and end apart: 6, of which 6 were waited for; matrix products, arithmetic and copies ran while one was open for 0% of the time, Pallas kernels for 0%

profile of v1, /device:TPU:67, one launch (start us, length us, event | category | flops | bytes accessed | tf_op | source)
XLA Modules:
  0.0 131.8 jit_solution(1406690700780378358)
XLA Ops:
  0.0 0.0 copy-start
  0.0 6.0 %shard_map.64 = f32[2,8,56,512]{3,2,1,0:T(8,128)} custom-call(s32[1]{0:T(128)} %bitcast.2.place_ref, bf16[768,1024]{1,0:T(8,128)(2,1)} %mine_ref.1, bf16[768,1024]{1,0:T(8,128)(2,1)} %mine_ref.1, bf16[1,501,1024]{2,1,0:T(8,128)(2,1)} %unembed_ref.1, bf16[1024,512]{1,0:T(8,128)(2,1)} %width_ref.1), custom_call_target="tpu_custom_call" | custom-call | tf_op jit(solution)/shard_map/pallas_call | solution.py:76
  6.1 8.8 %all-to-all-start = ((f32[16,56,512]{2,1,0:T(8,128)}), f32[16,56,512]{2,1,0:T(8,128)S(1)}, u32[]{:S(2)}, u32[]{:S(2)}) async-start(f32[16,56,512]{2,1,0:T(8,128)} %bitcast.8), calls=%async_computation | async-start | bytes 3670016 | tf_op jit(solution)/shard_map/all_to_all | solution.py:206
  14.9 0.1 pad_add_fusion.place_ref
  15.0 22.8 %all-to-all-done.pieces_ref = f32[16,56,512]{2,1,0:T(8,128)S(1)} async-done(((f32[16,56,512]{2,1,0:T(8,128)}), f32[16,56,512]{2,1,0:T(8,128)S(1)}, u32[]{:S(2)}, u32[]{:S(2)}) %all-to-all-start) | async-done | bytes 1835040 | tf_op jit(solution)/shard_map/all_to_all | solution.py:206
  37.8 1.0 shard_map.65
  38.8 0.0 copy-start.1
  38.8 12.1 %all-to-all-start.1 = ((f32[32,2,128]{2,1,0:T(2,128)}), f32[32,2,128]{2,1,0:T(2,128)S(1)}, u32[]{:S(2)}, u32[]{:S(2)}) async-start(f32[32,2,128]{2,1,0:T(2,128)} %get-tuple-element.12), calls=%async_computation.1 | async-start | bytes 65536 | tf_op jit(solution)/shard_map/all_to_all | solution.py:206
  50.9 3.1 %collective-permute-start = (f32[8,512]{1,0:T(8,128)S(1)}, f32[8,512]{1,0:T(8,128)S(1)}, u32[]{:S(2)}, u32[]{:S(2)}) collective-permute-start(f32[8,512]{1,0:T(8,128)S(1)} %get-tuple-element.14), channel_id=1, source_target_pairs={{0,8},{8,0},{1,9},{9,1},{2,10},{10,2},{3,11},{11,3},{4,12},{12,4},... | collective-permute-start | bytes 49160 | tf_op jit(solution)/shard_map/ppermute | solution.py:210
  53.9 0.0 copy-done
  54.0 0.1 dynamic-slice_bitcast_fusion
  54.0 0.1 copy.11.labels_ref
  54.1 0.6 collective-permute-done.got_ref
  54.8 7.2 %all-to-all-done.1.stats_ref = f32[32,2,128]{2,1,0:T(2,128)S(1)} async-done(((f32[32,2,128]{2,1,0:T(2,128)}), f32[32,2,128]{2,1,0:T(2,128)S(1)}, u32[]{:S(2)}, u32[]{:S(2)}) %all-to-all-start.1) | async-done | bytes 32800 | tf_op jit(solution)/shard_map/all_to_all | solution.py:206
  62.0 1.7 %shard_map.66 = bf16[8,112,512]{2,1,0:T(8,128)(2,1)} custom-call(s32[2]{0:T(128)S(1)} %pad_add_fusion.place_ref, f32[96,512]{1,0:T(8,128)S(1)} %get-tuple-element.11.logits_ref, f32[32,2,128]{2,1,0:T(2,128)S(1)} %all-to-all-done.1.stats_ref, s32[48,1]{1,0:T(8,128)S(1)} %copy.11.labels_ref, f32[8,512]{1,0:T(8,128)S(1)} %get-tuple-element.13.keep_ref, ...), custom_call_target="tpu_custom_call" | custom-call | tf_op jit(solution)/shard_map/pallas_call | solution.py:237
  63.7 5.5 %all-to-all-start.2 = ((bf16[8,112,512]{2,1,0:T(8,128)(2,1)}), bf16[8,112,512]{2,1,0:T(8,128)(2,1)S(1)}, u32[]{:S(2)}, u32[]{:S(2)}) async-start(bf16[8,112,512]{2,1,0:T(8,128)(2,1)} %shard_map.66), calls=%async_computation.2 | async-start | bytes 1835008 | tf_op jit(solution)/shard_map/all_to_all | solution.py:206
  69.2 0.0 copy-done.1
  69.2 0.0 copy-start.2
  69.2 4.6 %collective-permute-start.1 = (bf16[1,501,501]{2,1,0:T(8,128)(2,1)S(1)}, bf16[1,501,501]{2,1,0:T(8,128)(2,1)S(1)}, u32[]{:S(2)}, u32[]{:S(2)}) collective-permute-start(bf16[1,501,501]{2,1,0:T(8,128)(2,1)S(1)} %copy-done.1), channel_id=1, source_target_pairs={{0,8},{8,0},{1,9},{9,1},{2,10},{10,2},{3,11},{11,3},{4,12},{12,4},... | collective-permute-start | bytes 1506014 | tf_op jit(solution)/shard_map/ppermute | solution.py:210
  73.7 1.5 %collective-permute-done.1.other_ref = bf16[1,501,501]{2,1,0:T(8,128)(2,1)S(1)} collective-permute-done((bf16[1,501,501]{2,1,0:T(8,128)(2,1)S(1)}, bf16[1,501,501]{2,1,0:T(8,128)(2,1)S(1)}, u32[]{:S(2)}, u32[]{:S(2)}) %collective-permute-start.1) | collective-permute-done | bytes 502034 | tf_op jit(solution)/shard_map/ppermute | solution.py:210
  75.2 6.7 %all-to-all-done.2.packed_ref = bf16[8,112,512]{2,1,0:T(8,128)(2,1)S(1)} async-done(((bf16[8,112,512]{2,1,0:T(8,128)(2,1)}), bf16[8,112,512]{2,1,0:T(8,128)(2,1)S(1)}, u32[]{:S(2)}, u32[]{:S(2)}) %all-to-all-start.2) | async-done | bytes 917536 | tf_op jit(solution)/shard_map/all_to_all | solution.py:206
  82.0 1.5 %shard_map.67 = (bf16[4,96,512]{2,1,0:T(8,128)(2,1)S(1)}, bf16[8,96,512]{2,1,0:T(8,128)(2,1)}) custom-call(s32[1]{0:T(128)} %bitcast.core_ref, bf16[8,112,512]{2,1,0:T(8,128)(2,1)S(1)} %all-to-all-done.2.packed_ref, bf16[1,501,501]{2,1,0:T(8,128)(2,1)S(1)} %copy-done.1, bf16[1,501,501]{2,1,0:T(8,128)(2,1)S(1)} %collective-permute-done.1.other_ref), custom_call_target="tpu_custom_call" | custom-call | tf_op jit(solution)/shard_map/pallas_call | solution.py:242
  83.5 15.3 %all_to_all.25.pieces_ref = bf16[4,96,512]{2,1,0:T(8,128)(2,1)S(1)} all-to-all(bf16[4,96,512]{2,1,0:T(8,128)(2,1)S(1)} %get-tuple-element.15), channel_id=1, replica_groups=mesh['vocab'=8,'chip'=4,'core'=2,'width'=8] {'chip'}, dimensions={0} | all-to-all | bytes 786432 | tf_op jit(solution)/shard_map/all_to_all | solution.py:206
  98.8 3.5 %all-to-all-start.4 = ((bf16[8,96,512]{2,1,0:T(8,128)(2,1)}), bf16[8,96,512]{2,1,0:T(8,128)(2,1)S(1)}, u32[]{:S(2)}, u32[]{:S(2)}) async-start(bf16[8,96,512]{2,1,0:T(8,128)(2,1)} %get-tuple-element.16), calls=%async_computation.4 | async-start | bytes 1572864 | tf_op jit(solution)/shard_map/all_to_all | solution.py:206
  102.4 0.0 copy-done.2
  102.4 0.1 convert_reduce_fusion.starts_ref
  102.5 0.1 shard_map.68
  102.6 18.2 %all_gather.3.turned_ref = bf16[768,512]{1,0:T(8,128)(2,1)S(1)} all-gather(bf16[96,512]{1,0:T(8,128)(2,1)S(1)} %shard_map.68), channel_id=1, replica_groups=mesh['vocab'=8,'chip'=4,'core'=2,'width'=8] {'chip','core'}, dimensions={0}, use_global_device_ids=true | all-gather | bytes 884736 | tf_op jit(solution)/shard_map/all_gather | solution.py:249
  120.8 5.1 %all-to-all-done.4 = bf16[8,96,512]{2,1,0:T(8,128)(2,1)S(1)} async-done(((bf16[8,96,512]{2,1,0:T(8,128)(2,1)}), bf16[8,96,512]{2,1,0:T(8,128)(2,1)S(1)}, u32[]{:S(2)}, u32[]{:S(2)}) %all-to-all-start.4) | async-done | bytes 786464 | tf_op jit(solution)/shard_map/all_to_all | solution.py:206
  125.9 3.9 %shard_map.69 = f32[2004,128]{1,0:T(8,128)S(1)} custom-call(s32[13]{0:T(128)S(1)} %convert_reduce_fusion.starts_ref, bf16[768,512]{1,0:T(8,128)(2,1)S(1)} %all_gather.3.turned_ref, bf16[768,512]{1,0:T(8,128)(2,1)S(1)} %bitcast.7), custom_call_target="tpu_custom_call" | custom-call | tf_op jit(solution)/shard_map/pallas_call | solution.py:187
  129.8 2.0 %reshape.25 = f32[1,501,512]{2,0,1:T(1,128)} reshape(f32[2004,128]{1,0:T(8,128)S(1)} %shard_map.69) | data formatting | bytes 2052096 | tf_op jit(solution)/shard_map/reshape | solution.py:202
Async XLA Ops:
  0.0 53.9 %copy-start = (s32[768]{0:T(1024)S(1)}, s32[768]{0:T(1024)}, u32[]{:S(2)}) copy-start(s32[768]{0:T(1024)} %param.10) | copy-start | bytes 9220
  6.1 31.7 %all-to-all-start = ((f32[16,56,512]{2,1,0:T(8,128)}), f32[16,56,512]{2,1,0:T(8,128)S(1)}, u32[]{:S(2)}, u32[]{:S(2)}) async-start(f32[16,56,512]{2,1,0:T(8,128)} %bitcast.8), calls=%async_computation | async-start | bytes 3670016 | tf_op jit(solution)/shard_map/all_to_all | solution.py:206
  38.8 30.4 %copy-start.1 = (bf16[1,501,501]{2,1,0:T(8,128)(2,1)S(1)}, bf16[1,501,501]{2,1,0:T(8,128)(2,1)}, u32[]{:S(2)}) copy-start(bf16[1,501,501]{2,1,0:T(8,128)(2,1)} %basis_ref.1) | copy-start | bytes 1506010
  38.8 23.2 %all-to-all-start.1 = ((f32[32,2,128]{2,1,0:T(2,128)}), f32[32,2,128]{2,1,0:T(2,128)S(1)}, u32[]{:S(2)}, u32[]{:S(2)}) async-start(f32[32,2,128]{2,1,0:T(2,128)} %get-tuple-element.12), calls=%async_computation.1 | async-start | bytes 65536 | tf_op jit(solution)/shard_map/all_to_all | solution.py:206
  50.9 3.9 %collective-permute-start = (f32[8,512]{1,0:T(8,128)S(1)}, f32[8,512]{1,0:T(8,128)S(1)}, u32[]{:S(2)}, u32[]{:S(2)}) collective-permute-start(f32[8,512]{1,0:T(8,128)S(1)} %get-tuple-element.14), channel_id=1, source_target_pairs={{0,8},{8,0},{1,9},{9,1},{2,10},{10,2},{3,11},{11,3},{4,12},{12,4},... | collective-permute-start | bytes 49160 | tf_op jit(solution)/shard_map/ppermute | solution.py:210
  63.7 18.3 %all-to-all-start.2 = ((bf16[8,112,512]{2,1,0:T(8,128)(2,1)}), bf16[8,112,512]{2,1,0:T(8,128)(2,1)S(1)}, u32[]{:S(2)}, u32[]{:S(2)}) async-start(bf16[8,112,512]{2,1,0:T(8,128)(2,1)} %shard_map.66), calls=%async_computation.2 | async-start | bytes 1835008 | tf_op jit(solution)/shard_map/all_to_all | solution.py:206
  69.2 33.2 %copy-start.2 = (s32[768]{0:T(1024)S(1)}, s32[768]{0:T(1024)}, u32[]{:S(2)}) copy-start(s32[768]{0:T(1024)} %param.11) | copy-start | bytes 9220
  69.2 6.1 %collective-permute-start.1 = (bf16[1,501,501]{2,1,0:T(8,128)(2,1)S(1)}, bf16[1,501,501]{2,1,0:T(8,128)(2,1)S(1)}, u32[]{:S(2)}, u32[]{:S(2)}) collective-permute-start(bf16[1,501,501]{2,1,0:T(8,128)(2,1)S(1)} %copy-done.1), channel_id=1, source_target_pairs={{0,8},{8,0},{1,9},{9,1},{2,10},{10,2},{3,11},{11,3},{4,12},{12,4},... | collective-permute-start | bytes 1506014 | tf_op jit(solution)/shard_map/ppermute | solution.py:210
  98.8 27.0 %all-to-all-start.4 = ((bf16[8,96,512]{2,1,0:T(8,128)(2,1)}), bf16[8,96,512]{2,1,0:T(8,128)(2,1)S(1)}, u32[]{:S(2)}, u32[]{:S(2)}) async-start(bf16[8,96,512]{2,1,0:T(8,128)(2,1)} %get-tuple-element.16), calls=%async_computation.4 | async-start | bytes 1572864 | tf_op jit(solution)/shard_map/all_to_all | solution.py:206

commit v2 on v1

--- a/solution.py
+++ b/solution.py
@@ -46,46 +46,44 @@
     return (column == source(row)).astype(jnp.float32).astype(jnp.bfloat16)
 
 
+def owned(core, width):
+    return (width // CORES * CORES + core) * GROUP + width % CORES * BLOCK
+
+
 def partial_kernel(place_ref, hidden_ref, mine_ref, unembed_ref, width_ref, out_ref):
     rows = unembed_ref.shape[1]
-    cores, each = out_ref.shape[:2]
     logits = lax.dot_general(
         hidden_ref[...], unembed_ref[0], (((1,), (1,)), ((), ())), preferred_element_type=jnp.float32
     )
-    first = pl.program_id(0) * each
 
     def source(row):
-        piece, within = row // SHARE, lax.rem(row, SHARE)
-        owner = (first + lax.rem(piece, each)) * cores + piece // each
-        return jnp.where(within < DEALT, owner * DEALT + within, -1)
-
-    dealt = jnp.dot(pick((cores * each * SHARE, GROUP), source), mine_ref[...], preferred_element_type=jnp.float32)
+        core, width, within = row // (PARTS * SHARE), lax.rem(row // SHARE, PARTS), lax.rem(row, SHARE)
+        return jnp.where(within < DEALT, (width * CORES + core) * DEALT + within, -1)
+
+    dealt = jnp.dot(pick((CORES * PARTS * SHARE, GROUP), source), mine_ref[...], preferred_element_type=jnp.float32)
     projected = jnp.dot(dealt.astype(jnp.bfloat16), width_ref[...], preferred_element_type=jnp.float32)
-    for core in range(cores):
-        for width in range(each):
-            piece = core * each + width
-            out_ref[core, width, :BLOCK, rows:] = jnp.zeros((BLOCK, LANES - rows), jnp.float32)
-            out_ref[core, width, :BLOCK, :rows] = logits[piece * BLOCK : (piece + 1) * BLOCK]
-            out_ref[core, width, BLOCK:, :] = projected[piece * SHARE : (piece + 1) * SHARE]
+    for core in range(CORES):
+        for width in range(PARTS):
+            owner, begin = core * PARTS + width, owned(core, width)
+            out_ref[owner, :BLOCK, rows:] = jnp.zeros((BLOCK, LANES - rows), jnp.float32)
+            out_ref[owner, :BLOCK, :rows] = logits[begin : begin + BLOCK]
+            out_ref[owner, BLOCK:, :] = projected[owner * SHARE : (owner + 1) * SHARE]
 
 
 def partial_sums(place, hidden, unembed, rotate_width):
-    each = PARTS // CHIPS
-    features, columns = rotate_width.shape
-    rows = unembed.shape[1]
     return pl.pallas_call(
         partial_kernel,
-        out_shape=jax.ShapeDtypeStruct((CORES, PARTS, ROWS, LANES), jnp.float32),
+        out_shape=jax.ShapeDtypeStruct((CORES * PARTS, ROWS, LANES), jnp.float32),
         grid_spec=pltpu.PrefetchScalarGridSpec(
             num_scalar_prefetch=1,
-            grid=(CHIPS,),
+            grid=(1,),
             in_specs=[
-                pl.BlockSpec((CORES * GROUP, features), lambda g, place: (g, 0)),
-                pl.BlockSpec((GROUP, features), lambda g, place: (place[0], 0)),
-                pl.BlockSpec((1, rows, features), lambda g, place: (0, 0, 0)),
-                pl.BlockSpec((features, columns), lambda g, place: (0, 0)),
+                pl.BlockSpec(hidden.shape, lambda g, place: (0, 0)),
+                pl.BlockSpec((GROUP, hidden.shape[1]), lambda g, place: (place[0], 0)),
+                pl.BlockSpec(unembed.shape, lambda g, place: (0, 0, 0)),
+                pl.BlockSpec(rotate_width.shape, lambda g, place: (0, 0)),
             ],
-            out_specs=pl.BlockSpec((CORES, each, ROWS, LANES), lambda g, place: (0, g, 0, 0)),
+            out_specs=pl.BlockSpec((CORES * PARTS, ROWS, LANES), lambda g, place: (0, 0, 0)),
         ),
         compiler_params=pltpu.CompilerParams(vmem_limit_bytes=MOST),
     )(place, hidden, hidden, unembed, rotate_width)
@@ -134,7 +132,7 @@
         out_ref[piece, CORES * BLOCK :] = share
 
 
-def turn_kernel(core_ref, packed_ref, basis_ref, other_ref, out_ref, share_ref):
+def turn_kernel(core_ref, packed_ref, basis_ref, other_ref, starts_ref, out_ref, share_ref):
     rows = basis_ref.shape[1]
     turned = 0.0
     for core, ref in ((core_ref[0], basis_ref), (1 - core_ref[0], other_ref)):
@@ -174,19 +172,15 @@
         elif sequence < SEQS - 1:
             total_ref[...] += gradient * gradient
         else:
-            total = total_ref[...] + gradient * gradient
-            tile, width = total.shape
-            pieces = width // 128
-            for piece in range(pieces):
-                out_ref[pl.ds(piece, tile, stride=pieces), :] = total[:, piece * 128 : (piece + 1) * 128]
+            out_ref[...] = (total_ref[...] + gradient * gradient).reshape(out_ref.shape)
 
 
 def gradients(starts, turned, projected, height):
     width = projected.shape[1]
-    tile, pieces = 128, width // 128
-    flat = pl.pallas_call(
+    tile = 256
+    out = pl.pallas_call(
         gradient_kernel,
-        out_shape=jax.ShapeDtypeStruct((height * pieces, 128), jnp.float32),
+        out_shape=jax.ShapeDtypeStruct((height, 1, width), jnp.float32),
         grid_spec=pltpu.PrefetchScalarGridSpec(
             num_scalar_prefetch=1,
             grid=(LANES // tile,),
@@ -194,12 +188,12 @@
                 pl.BlockSpec((TOKENS, tile), lambda g, starts: (0, g)),
                 pl.BlockSpec((TOKENS, width), lambda g, starts: (0, 0)),
             ],
-            out_specs=pl.BlockSpec((tile * pieces, 128), lambda g, starts: (g, 0)),
+            out_specs=pl.BlockSpec((tile, 1, width), lambda g, starts: (g, 0, 0)),
             scratch_shapes=[pltpu.VMEM((tile, width), jnp.float32)],
         ),
-        compiler_params=pltpu.CompilerParams(vmem_limit_bytes=VMEM),
+        compiler_params=pltpu.CompilerParams(vmem_limit_bytes=16 * 1024 * 1024),
     )(starts, turned, projected)
-    return flat.reshape(1, height, width)
+    return out.transpose(1, 0, 2)
 
 
 def exchange(values, axis):
@@ -215,14 +209,13 @@
     vocab, chip, core, width = (lax.axis_index(a).astype(jnp.int32) for a in ("vocab", "chip", "core", "width"))
     place = jnp.stack([core, (vocab * PARTS + chip * CORES) * rows])
     core = core.reshape(1)
-    owned = (width // CORES * CORES + core[0]) * GROUP + lax.rem(width, CORES) * BLOCK
-    mine = lax.dynamic_slice_in_dim(labels, owned, BLOCK, 0).reshape(BLOCK, 1)
+    mine = lax.dynamic_slice_in_dim(labels, owned(core[0], width), BLOCK, 0).reshape(BLOCK, 1)
     sequence_index = jnp.arange(SEQS + 1, dtype=jnp.int32)
     starts = jnp.sum((seq_ids[None, :] < sequence_index[:, None]).astype(jnp.int32), axis=1)
     half, single = jnp.bfloat16, jnp.float32
 
     pieces = partial_sums(vocab.reshape(1), hidden, unembed, rotate_width)
-    pieces = exchange(pieces.reshape(CORES * PARTS, ROWS, LANES), ("core", "width"))
+    pieces = exchange(pieces, ("core", "width"))
     logits, stats, keep, send = call(
         functools.partial(local_kernel, rows),
         [
@@ -242,8 +235,8 @@
     turned, share = call(
         turn_kernel,
         [((CHIPS, GROUP, LANES), half), ((PARTS, GROUP, LANES), half)],
-        [SCALARS, FULL, FULL, FULL],
-    )(core, exchange(packed, "width"), rotate_vocab, swap(rotate_vocab))
+        [SCALARS, FULL, FULL, FULL, pl.BlockSpec(memory_space=pl.ANY)],
+    )(core, exchange(packed, "width"), rotate_vocab, swap(rotate_vocab), starts)
     projected = exchange(share, "vocab").reshape(TOKENS, LANES)
     turned = call(sum_kernel, [((GROUP, LANES), half)], [FULL])(exchange(turned, "chip"))
     turned = lax.all_gather(turned, ROW, axis=0, tiled=True)

time: 132 us -> 129 us (0.977)
  local copies, waits for them, and re-layouts: 2.15 us -> 0.19 us
  Pallas kernels: 14.3 us -> 12.8 us
    reshape x3 -> x2, local copies, waits for them, and re-layouts: 2.14 us -> 0.17 us  [body(): lax.dynamic_slice_in_dim(labels, owned(core[0], width), BLOCK, 0)]
    pallas_call x2, Pallas kernels: 9.99 us -> 8.44 us  [the longest x1 4.71 us: partial_sums(): pl.pallas_call(partial_kernel, out_shape=jax.ShapeDtypeStruct((CORES * PA...]
where the time goes in v2:
time: 129 us; the launch traced here: 128 us
  waiting for transfers between devices  44.1 us (34%)
  starting transfers between devices  37.4 us (29%)
  blocking collectives  33.6 us (26%)
  Pallas kernels  12.8 us (10%)
    all_to_all x4, waiting for transfers between devices, exchange(): return lax.all_to_all(values, axis, 0, 0, tiled=True)  42.1 us
    all_to_all x4, starting transfers between devices, exchange(): return lax.all_to_all(values, axis, 0, 0, tiled=True)  29.9 us
    all_gather x1, blocking collectives, body(): turned = lax.all_gather(turned, ROW, axis=0, tiled=True)  18.2 us
    all_to_all x1, blocking collectives, exchange(): return lax.all_to_all(values, axis, 0, 0, tiled=True)  15.4 us
    ppermute x2, starting transfers between devices, swap(): lax.ppermute(values, 'core', [(i, CORES - 1 - i) for i in range(CORES)])  7.49 us
    pallas_call x1, Pallas kernels, partial_sums(): pl.pallas_call(partial_kernel, out_shape=jax.ShapeDtypeStruct((CORES * PA...  4.71 us
    pallas_call x1, Pallas kernels, gradients(): pl.pallas_call(gradient_kernel, out_shape=jax.ShapeDtypeStruct((height, 1...  3.73 us
  transfers between devices with their start and end apart: 6, of which 6 were waited for; matrix products, arithmetic and copies ran while one was open for 0% of the time, Pallas kernels for 0%

profile of v2, /device:TPU:67, one launch (start us, length us, event | category | flops | bytes accessed | tf_op | source)
XLA Modules:
  0.0 128.3 jit_solution(8907044570826705589)
XLA Ops:
  0.0 0.0 copy-start
  0.0 4.7 %shard_map.64 = f32[16,56,512]{2,1,0:T(8,128)} custom-call(s32[1]{0:T(128)} %bitcast.2.place_ref, bf16[768,1024]{1,0:T(8,128)(2,1)} %mine_ref.1, bf16[768,1024]{1,0:T(8,128)(2,1)} %mine_ref.1, bf16[1,501,1024]{2,1,0:T(8,128)(2,1)} %unembed_ref.1, bf16[1024,512]{1,0:T(8,128)(2,1)} %width_ref.1), custom_call_target="tpu_custom_call" | custom-call | tf_op jit(solution)/shard_map/pallas_call | solution.py:74
  4.7 8.9 %all-to-all-start = ((f32[16,56,512]{2,1,0:T(8,128)}), f32[16,56,512]{2,1,0:T(8,128)S(1)}, u32[]{:S(2)}, u32[]{:S(2)}) async-start(f32[16,56,512]{2,1,0:T(8,128)} %shard_map.64), calls=%async_computation | async-start | bytes 3670016 | tf_op jit(solution)/shard_map/all_to_all | solution.py:200
  13.6 0.1 pad_add_fusion.place_ref
  13.6 22.8 %all-to-all-done.pieces_ref = f32[16,56,512]{2,1,0:T(8,128)S(1)} async-done(((f32[16,56,512]{2,1,0:T(8,128)}), f32[16,56,512]{2,1,0:T(8,128)S(1)}, u32[]{:S(2)}, u32[]{:S(2)}) %all-to-all-start) | async-done | bytes 1835040 | tf_op jit(solution)/shard_map/all_to_all | solution.py:200
  36.5 1.0 shard_map.65
  37.5 0.0 copy-start.1
  37.5 0.0 copy-start.2
  37.5 12.1 %all-to-all-start.1 = ((f32[32,2,128]{2,1,0:T(2,128)}), f32[32,2,128]{2,1,0:T(2,128)S(1)}, u32[]{:S(2)}, u32[]{:S(2)}) async-start(f32[32,2,128]{2,1,0:T(2,128)} %get-tuple-element.12), calls=%async_computation.1 | async-start | bytes 65536 | tf_op jit(solution)/shard_map/all_to_all | solution.py:200
  49.6 3.1 %collective-permute-start = (f32[8,512]{1,0:T(8,128)S(1)}, f32[8,512]{1,0:T(8,128)S(1)}, u32[]{:S(2)}, u32[]{:S(2)}) collective-permute-start(f32[8,512]{1,0:T(8,128)S(1)} %get-tuple-element.14), channel_id=1, source_target_pairs={{0,8},{8,0},{1,9},{9,1},{2,10},{10,2},{3,11},{11,3},{4,12},{12,4},... | collective-permute-start | bytes 49160 | tf_op jit(solution)/shard_map/ppermute | solution.py:204
  52.6 0.0 copy-done
  52.6 0.1 dynamic-slice_bitcast_fusion
  52.7 0.1 copy.8.labels_ref
  52.8 0.6 collective-permute-done.got_ref
  53.4 7.2 %all-to-all-done.1.stats_ref = f32[32,2,128]{2,1,0:T(2,128)S(1)} async-done(((f32[32,2,128]{2,1,0:T(2,128)}), f32[32,2,128]{2,1,0:T(2,128)S(1)}, u32[]{:S(2)}, u32[]{:S(2)}) %all-to-all-start.1) | async-done | bytes 32800 | tf_op jit(solution)/shard_map/all_to_all | solution.py:200
  60.7 1.7 %shard_map.66 = bf16[8,112,512]{2,1,0:T(8,128)(2,1)} custom-call(s32[2]{0:T(128)S(1)} %pad_add_fusion.place_ref, f32[96,512]{1,0:T(8,128)S(1)} %get-tuple-element.11.logits_ref, f32[32,2,128]{2,1,0:T(2,128)S(1)} %all-to-all-done.1.stats_ref, s32[48,1]{1,0:T(8,128)S(1)} %copy.8.labels_ref, f32[8,512]{1,0:T(8,128)S(1)} %get-tuple-element.13.keep_ref, ...), custom_call_target="tpu_custom_call" | custom-call | tf_op jit(solution)/shard_map/pallas_call | solution.py:230
  62.4 5.5 %all-to-all-start.2 = ((bf16[8,112,512]{2,1,0:T(8,128)(2,1)}), bf16[8,112,512]{2,1,0:T(8,128)(2,1)S(1)}, u32[]{:S(2)}, u32[]{:S(2)}) async-start(bf16[8,112,512]{2,1,0:T(8,128)(2,1)} %shard_map.66), calls=%async_computation.2 | async-start | bytes 1835008 | tf_op jit(solution)/shard_map/all_to_all | solution.py:200
  67.8 0.0 copy-done.1
  67.8 4.4 %collective-permute-start.1 = (bf16[1,501,501]{2,1,0:T(8,128)(2,1)S(1)}, bf16[1,501,501]{2,1,0:T(8,128)(2,1)S(1)}, u32[]{:S(2)}, u32[]{:S(2)}) collective-permute-start(bf16[1,501,501]{2,1,0:T(8,128)(2,1)S(1)} %copy-done.1), channel_id=1, source_target_pairs={{0,8},{8,0},{1,9},{9,1},{2,10},{10,2},{3,11},{11,3},{4,12},{12,4},... | collective-permute-start | bytes 1506014 | tf_op jit(solution)/shard_map/ppermute | solution.py:204
  72.3 0.0 copy-done.2
  72.3 0.1 convert_reduce_fusion.starts_ref
  72.4 1.4 %collective-permute-done.1.other_ref = bf16[1,501,501]{2,1,0:T(8,128)(2,1)S(1)} collective-permute-done((bf16[1,501,501]{2,1,0:T(8,128)(2,1)S(1)}, bf16[1,501,501]{2,1,0:T(8,128)(2,1)S(1)}, u32[]{:S(2)}, u32[]{:S(2)}) %collective-permute-start.1) | collective-permute-done | bytes 502034 | tf_op jit(solution)/shard_map/ppermute | solution.py:204
  73.8 6.9 %all-to-all-done.2.packed_ref = bf16[8,112,512]{2,1,0:T(8,128)(2,1)S(1)} async-done(((bf16[8,112,512]{2,1,0:T(8,128)(2,1)}), bf16[8,112,512]{2,1,0:T(8,128)(2,1)S(1)}, u32[]{:S(2)}, u32[]{:S(2)}) %all-to-all-start.2) | async-done | bytes 917536 | tf_op jit(solution)/shard_map/all_to_all | solution.py:200
  80.6 1.5 %shard_map.67 = (bf16[4,96,512]{2,1,0:T(8,128)(2,1)S(1)}, bf16[8,96,512]{2,1,0:T(8,128)(2,1)}) custom-call(s32[1]{0:T(128)} %bitcast.core_ref, bf16[8,112,512]{2,1,0:T(8,128)(2,1)S(1)} %all-to-all-done.2.packed_ref, bf16[1,501,501]{2,1,0:T(8,128)(2,1)S(1)} %copy-done.1, bf16[1,501,501]{2,1,0:T(8,128)(2,1)S(1)} %collective-permute-done.1.other_ref, ...), custom_call_target="tpu_custom_call" | custom-call | tf_op jit(solution)/shard_map/pallas_call | solution.py:235
  82.2 15.4 %all_to_all.25.pieces_ref = bf16[4,96,512]{2,1,0:T(8,128)(2,1)S(1)} all-to-all(bf16[4,96,512]{2,1,0:T(8,128)(2,1)S(1)} %get-tuple-element.15), channel_id=1, replica_groups=mesh['vocab'=8,'chip'=4,'core'=2,'width'=8] {'chip'}, dimensions={0} | all-to-all | bytes 786432 | tf_op jit(solution)/shard_map/all_to_all | solution.py:200
  97.6 3.5 %all-to-all-start.4 = ((bf16[8,96,512]{2,1,0:T(8,128)(2,1)}), bf16[8,96,512]{2,1,0:T(8,128)(2,1)S(1)}, u32[]{:S(2)}, u32[]{:S(2)}) async-start(bf16[8,96,512]{2,1,0:T(8,128)(2,1)} %get-tuple-element.16), calls=%async_computation.4 | async-start | bytes 1572864 | tf_op jit(solution)/shard_map/all_to_all | solution.py:200
  101.1 0.1 shard_map.68
  101.2 18.2 %all_gather.3.turned_ref = bf16[768,512]{1,0:T(8,128)(2,1)S(1)} all-gather(bf16[96,512]{1,0:T(8,128)(2,1)S(1)} %shard_map.68), channel_id=1, replica_groups=mesh['vocab'=8,'chip'=4,'core'=2,'width'=8] {'chip','core'}, dimensions={0}, use_global_device_ids=true | all-gather | bytes 884736 | tf_op jit(solution)/shard_map/all_gather | solution.py:242
  119.4 5.2 %all-to-all-done.4 = bf16[8,96,512]{2,1,0:T(8,128)(2,1)S(1)} async-done(((bf16[8,96,512]{2,1,0:T(8,128)(2,1)}), bf16[8,96,512]{2,1,0:T(8,128)(2,1)S(1)}, u32[]{:S(2)}, u32[]{:S(2)}) %all-to-all-start.4) | async-done | bytes 786464 | tf_op jit(solution)/shard_map/all_to_all | solution.py:200
  124.6 3.7 %shard_map.69 = f32[501,1,512]{2,1,0:T(1,128)} custom-call(s32[13]{0:T(128)S(1)} %convert_reduce_fusion.starts_ref, bf16[768,512]{1,0:T(8,128)(2,1)S(1)} %all_gather.3.turned_ref, bf16[768,512]{1,0:T(8,128)(2,1)S(1)} %bitcast.7), custom_call_target="tpu_custom_call" | custom-call | tf_op jit(solution)/shard_map/pallas_call | solution.py:181
Async XLA Ops:
  0.0 52.6 %copy-start = (s32[768]{0:T(1024)S(1)}, s32[768]{0:T(1024)}, u32[]{:S(2)}) copy-start(s32[768]{0:T(1024)} %param.10) | copy-start | bytes 9220
  4.7 31.7 %all-to-all-start = ((f32[16,56,512]{2,1,0:T(8,128)}), f32[16,56,512]{2,1,0:T(8,128)S(1)}, u32[]{:S(2)}, u32[]{:S(2)}) async-start(f32[16,56,512]{2,1,0:T(8,128)} %shard_map.64), calls=%async_computation | async-start | bytes 3670016 | tf_op jit(solution)/shard_map/all_to_all | solution.py:200
  37.5 30.4 %copy-start.1 = (bf16[1,501,501]{2,1,0:T(8,128)(2,1)S(1)}, bf16[1,501,501]{2,1,0:T(8,128)(2,1)}, u32[]{:S(2)}) copy-start(bf16[1,501,501]{2,1,0:T(8,128)(2,1)} %basis_ref.1) | copy-start | bytes 1506010
  37.5 34.8 %copy-start.2 = (s32[768]{0:T(1024)S(1)}, s32[768]{0:T(1024)}, u32[]{:S(2)}) copy-start(s32[768]{0:T(1024)} %param.11) | copy-start | bytes 9220
  37.5 23.2 %all-to-all-start.1 = ((f32[32,2,128]{2,1,0:T(2,128)}), f32[32,2,128]{2,1,0:T(2,128)S(1)}, u32[]{:S(2)}, u32[]{:S(2)}) async-start(f32[32,2,128]{2,1,0:T(2,128)} %get-tuple-element.12), calls=%async_computation.1 | async-start | bytes 65536 | tf_op jit(solution)/shard_map/all_to_all | solution.py:200
  49.6 3.9 %collective-permute-start = (f32[8,512]{1,0:T(8,128)S(1)}, f32[8,512]{1,0:T(8,128)S(1)}, u32[]{:S(2)}, u32[]{:S(2)}) collective-permute-start(f32[8,512]{1,0:T(8,128)S(1)} %get-tuple-element.14), channel_id=1, source_target_pairs={{0,8},{8,0},{1,9},{9,1},{2,10},{10,2},{3,11},{11,3},{4,12},{12,4},... | collective-permute-start | bytes 49160 | tf_op jit(solution)/shard_map/ppermute | solution.py:204
  62.4 18.3 %all-to-all-start.2 = ((bf16[8,112,512]{2,1,0:T(8,128)(2,1)}), bf16[8,112,512]{2,1,0:T(8,128)(2,1)S(1)}, u32[]{:S(2)}, u32[]{:S(2)}) async-start(bf16[8,112,512]{2,1,0:T(8,128)(2,1)} %shard_map.66), calls=%async_computation.2 | async-start | bytes 1835008 | tf_op jit(solution)/shard_map/all_to_all | solution.py:200
  67.8 5.9 %collective-permute-start.1 = (bf16[1,501,501]{2,1,0:T(8,128)(2,1)S(1)}, bf16[1,501,501]{2,1,0:T(8,128)(2,1)S(1)}, u32[]{:S(2)}, u32[]{:S(2)}) collective-permute-start(bf16[1,501,501]{2,1,0:T(8,128)(2,1)S(1)} %copy-done.1), channel_id=1, source_target_pairs={{0,8},{8,0},{1,9},{9,1},{2,10},{10,2},{3,11},{11,3},{4,12},{12,4},... | collective-permute-start | bytes 1506014 | tf_op jit(solution)/shard_map/ppermute | solution.py:204
  97.6 27.0 %all-to-all-start.4 = ((bf16[8,96,512]{2,1,0:T(8,128)(2,1)}), bf16[8,96,512]{2,1,0:T(8,128)(2,1)S(1)}, u32[]{:S(2)}, u32[]{:S(2)}) async-start(bf16[8,96,512]{2,1,0:T(8,128)(2,1)} %get-tuple-element.16), calls=%async_computation.4 | async-start | bytes 1572864 | tf_op jit(solution)/shard_map/all_to_all | solution.py:200

commit v3 on v2

--- a/solution.py
+++ b/solution.py
@@ -19,6 +19,7 @@
 DEALT = BLOCK // PARTS
 SHARE = 8
 ROWS = BLOCK + SHARE
+SENT = 16
 LANES = 512
 WINDOW = SEQ_LEN + 16
 VMEM = 48 * 1024 * 1024
@@ -50,6 +51,24 @@
     return (width // CORES * CORES + core) * GROUP + width % CORES * BLOCK
 
 
+def step_of(exponent):
+    return jnp.exp2(exponent)
+
+
+def encode(values):
+    top, low = jnp.max(values, axis=1, keepdims=True), jnp.min(values, axis=1, keepdims=True)
+    middle, radius = 0.5 * top + 0.5 * low, 0.5 * top - 0.5 * low
+    least = jnp.maximum(jnp.maximum(radius / 32000.0, jnp.abs(middle) * 2.0**-29), 2.0**-100)
+    exponent = jnp.ceil(jnp.log2(least))
+    step = step_of(exponent)
+    offset = jnp.floor(middle / step + 0.5)
+    return jnp.floor((values - offset * step) / step + 0.5), exponent, offset
+
+
+def whole(values):
+    return values.astype(jnp.int32).astype(jnp.int16)
+
+
 def partial_kernel(place_ref, hidden_ref, mine_ref, unembed_ref, width_ref, out_ref):
     rows = unembed_ref.shape[1]
     logits = lax.dot_general(
@@ -57,23 +76,37 @@
     )
 
     def source(row):
-        core, width, within = row // (PARTS * SHARE), lax.rem(row // SHARE, PARTS), lax.rem(row, SHARE)
+        core, width, within = row // (PARTS * SENT), lax.rem(row // SENT, PARTS), lax.rem(row, SENT)
         return jnp.where(within < DEALT, (width * CORES + core) * DEALT + within, -1)
 
-    dealt = jnp.dot(pick((CORES * PARTS * SHARE, GROUP), source), mine_ref[...], preferred_element_type=jnp.float32)
+    dealt = jnp.dot(pick((CORES * PARTS * SENT, GROUP), source), mine_ref[...], preferred_element_type=jnp.float32)
     projected = jnp.dot(dealt.astype(jnp.bfloat16), width_ref[...], preferred_element_type=jnp.float32)
+    projected, share_exponent, share_offset = encode(projected)
+    logits, exponent, offset = encode(logits)
+    high = jnp.floor(offset / 32768.0)
+    share_high = jnp.floor(share_offset / 32768.0)
+    lane = lax.broadcasted_iota(jnp.int32, (BLOCK, LANES - rows), 1)
     for core in range(CORES):
         for width in range(PARTS):
             owner, begin = core * PARTS + width, owned(core, width)
-            out_ref[owner, :BLOCK, rows:] = jnp.zeros((BLOCK, LANES - rows), jnp.float32)
-            out_ref[owner, :BLOCK, :rows] = logits[begin : begin + BLOCK]
-            out_ref[owner, BLOCK:, :] = projected[owner * SHARE : (owner + 1) * SHARE]
+            tokens, shares = slice(begin, begin + BLOCK), slice(owner * SENT, (owner + 1) * SENT)
+            notes = jnp.where(lane == 0, exponent[tokens], 0.0)
+            notes = jnp.where(lane == 1, high[tokens], notes)
+            notes = jnp.where(lane == 2, offset[tokens] - high[tokens] * 32768.0, notes)
+            rest = jnp.zeros((BLOCK - SENT, 1), jnp.float32)
+            for number, part in enumerate(
+                (share_exponent[shares], share_high[shares], share_offset[shares] - share_high[shares] * 32768.0)
+            ):
+                notes = jnp.where(lane == 3 + number, jnp.concatenate([part, rest], axis=0), notes)
+            out_ref[owner, :BLOCK, :rows] = whole(logits[tokens])
+            out_ref[owner, :BLOCK, rows:] = whole(notes)
+            out_ref[owner, BLOCK:, :] = whole(projected[shares])
 
 
 def partial_sums(place, hidden, unembed, rotate_width):
     return pl.pallas_call(
         partial_kernel,
-        out_shape=jax.ShapeDtypeStruct((CORES * PARTS, ROWS, LANES), jnp.float32),
+        out_shape=jax.ShapeDtypeStruct((CORES * PARTS, BLOCK + SENT, LANES), jnp.int16),
         grid_spec=pltpu.PrefetchScalarGridSpec(
             num_scalar_prefetch=1,
             grid=(1,),
@@ -83,14 +116,25 @@
                 pl.BlockSpec(unembed.shape, lambda g, place: (0, 0, 0)),
                 pl.BlockSpec(rotate_width.shape, lambda g, place: (0, 0)),
             ],
-            out_specs=pl.BlockSpec((CORES * PARTS, ROWS, LANES), lambda g, place: (0, 0, 0)),
+            out_specs=pl.BlockSpec((CORES * PARTS, BLOCK + SENT, LANES), lambda g, place: (0, 0, 0)),
         ),
         compiler_params=pltpu.CompilerParams(vmem_limit_bytes=MOST),
     )(place, hidden, hidden, unembed, rotate_width)
 
 
+def decode(rows, pieces_ref, owner):
+    values = pieces_ref[owner].astype(jnp.int32).astype(jnp.float32)
+    notes = values[:BLOCK, rows:]
+    step = step_of(notes[:, 0:1])
+    logits = values[:BLOCK] * step + (notes[:, 1:2] * 32768.0 + notes[:, 2:3]) * step
+    notes = notes[:SHARE]
+    step = step_of(notes[:, 3:4])
+    share = values[BLOCK : BLOCK + SHARE] * step + (notes[:, 4:5] * 32768.0 + notes[:, 5:6]) * step
+    return jnp.concatenate([logits, share], axis=0)
+
+
 def local_kernel(rows, core_ref, pieces_ref, logits_ref, stats_ref, keep_ref, send_ref):
-    sums = [jnp.sum(pieces_ref[core * PARTS : (core + 1) * PARTS], axis=0) for core in range(CORES)]
+    sums = [sum(decode(rows, pieces_ref, core * PARTS + width) for width in range(PARTS)) for core in range(CORES)]
     column = lax.broadcasted_iota(jnp.int32, (CORES * BLOCK, LANES), 1)
     logits = jnp.concatenate([part[:BLOCK] for part in sums], axis=0)
     logits = jnp.where(column < rows, logits, -jnp.inf)

time: 129 us -> 125 us (0.969)
  the two profiles are of different devices: /device:TPU:67 before, /device:TPU:66 now
where the time goes in v3:
time: 125 us
  waiting for transfers between devices  42.7 us (34%)
  starting transfers between devices  33.9 us (27%)
  blocking collectives  33 us (26%)
  Pallas kernels  14.6 us (12%)
    all_to_all x4, waiting for transfers between devices, exchange(): return lax.all_to_all(values, axis, 0, 0, tiled=True)  40.9 us
    all_to_all x4, starting transfers between devices, exchange(): return lax.all_to_all(values, axis, 0, 0, tiled=True)  29.9 us
    all_gather x1, blocking collectives, body(): turned = lax.all_gather(turned, ROW, axis=0, tiled=True)  16.5 us
    all_to_all x1, blocking collectives, exchange(): return lax.all_to_all(values, axis, 0, 0, tiled=True)  16.5 us
    pallas_call x1, Pallas kernels, partial_sums(): pl.pallas_call(partial_kernel, out_shape=jax.ShapeDtypeStruct((CORES * PA...  5.35 us
    ppermute x2, starting transfers between devices, swap(): lax.ppermute(values, 'core', [(i, CORES - 1 - i) for i in range(CORES)])  3.95 us
    pallas_call x1, Pallas kernels, gradients(): pl.pallas_call(gradient_kernel, out_shape=jax.ShapeDtypeStruct((height, 1...  3.73 us
  transfers between devices with their start and end apart: 6, of which 5 were waited for; matrix products, arithmetic and copies ran while one was open for 0% of the time, Pallas kernels for 0%

profile of v3, /device:TPU:66, one launch (start us, length us, event | category | flops | bytes accessed | tf_op | source)
XLA Modules:
  0.0 124.6 jit_solution(11900721979607539216)
XLA Ops:
  0.0 0.0 copy-start
  0.0 5.4 %shard_map.64 = s16[16,64,512]{2,1,0:T(8,128)(2,1)} custom-call(s32[1]{0:T(128)} %bitcast.2.place_ref, bf16[768,1024]{1,0:T(8,128)(2,1)} %mine_ref.1, bf16[768,1024]{1,0:T(8,128)(2,1)} %mine_ref.1, bf16[1,501,1024]{2,1,0:T(8,128)(2,1)} %unembed_ref.1, bf16[1024,512]{1,0:T(8,128)(2,1)} %width_ref.1), custom_call_target="tpu_custom_call" | custom-call | tf_op jit(solution)/shard_map/pallas_call | solution.py:107
  5.4 8.5 %all-to-all-start = ((s16[16,64,512]{2,1,0:T(8,128)(2,1)}), s16[16,64,512]{2,1,0:T(8,128)(2,1)S(1)}, u32[]{:S(2)}, u32[]{:S(2)}) async-start(s16[16,64,512]{2,1,0:T(8,128)(2,1)} %shard_map.64), calls=%async_computation | async-start | bytes 2097152 | tf_op jit(solution)/shard_map/all_to_all | solution.py:244
  13.8 0.1 pad_add_fusion.place_ref
  13.9 14.5 %all-to-all-done.pieces_ref = s16[16,64,512]{2,1,0:T(8,128)(2,1)S(1)} async-done(((s16[16,64,512]{2,1,0:T(8,128)(2,1)}), s16[16,64,512]{2,1,0:T(8,128)(2,1)S(1)}, u32[]{:S(2)}, u32[]{:S(2)}) %all-to-all-start) | async-done | bytes 1048608 | tf_op jit(solution)/shard_map/all_to_all | solution.py:244
  28.4 2.2 %shard_map.65 = (f32[96,512]{1,0:T(8,128)S(1)}, f32[32,2,128]{2,1,0:T(2,128)}, f32[8,512]{1,0:T(8,128)S(1)}, f32[8,512]{1,0:T(8,128)S(1)}) custom-call(s32[1]{0:T(128)} %bitcast.core_ref, s16[16,64,512]{2,1,0:T(8,128)(2,1)S(1)} %all-to-all-done.pieces_ref), custom_call_target="tpu_custom_call" | custom-call | tf_op jit(solution)/shard_map/pallas_call | solution.py:263
  30.6 0.0 copy-start.1
  30.6 0.0 copy-start.2
  30.6 2.0 %collective-permute-start = (f32[8,512]{1,0:T(8,128)S(1)}, f32[8,512]{1,0:T(8,128)S(1)}, u32[]{:S(2)}, u32[]{:S(2)}) collective-permute-start(f32[8,512]{1,0:T(8,128)S(1)} %get-tuple-element.14), channel_id=1, source_target_pairs={{0,8},{8,0},{1,9},{9,1},{2,10},{10,2},{3,11},{11,3},{4,12},{12,4},... | collective-permute-start | bytes 49160 | tf_op jit(solution)/shard_map/ppermute | solution.py:248
  32.7 12.3 %all-to-all-start.1 = ((f32[32,2,128]{2,1,0:T(2,128)}), f32[32,2,128]{2,1,0:T(2,128)S(1)}, u32[]{:S(2)}, u32[]{:S(2)}) async-start(f32[32,2,128]{2,1,0:T(2,128)} %get-tuple-element.12), calls=%async_computation.1 | async-start | bytes 65536 | tf_op jit(solution)/shard_map/all_to_all | solution.py:244
  45.0 0.0 copy-done
  45.0 0.1 dynamic-slice_bitcast_fusion
  45.1 0.1 copy.8.labels_ref
  45.2 0.0 collective-permute-done.got_ref
  45.2 12.0 %all-to-all-done.1.stats_ref = f32[32,2,128]{2,1,0:T(2,128)S(1)} async-done(((f32[32,2,128]{2,1,0:T(2,128)}), f32[32,2,128]{2,1,0:T(2,128)S(1)}, u32[]{:S(2)}, u32[]{:S(2)}) %all-to-all-start.1) | async-done | bytes 32800 | tf_op jit(solution)/shard_map/all_to_all | solution.py:244
  57.2 1.7 %shard_map.66 = bf16[8,112,512]{2,1,0:T(8,128)(2,1)} custom-call(s32[2]{0:T(128)S(1)} %pad_add_fusion.place_ref, f32[96,512]{1,0:T(8,128)S(1)} %get-tuple-element.11.logits_ref, f32[32,2,128]{2,1,0:T(2,128)S(1)} %all-to-all-done.1.stats_ref, s32[48,1]{1,0:T(8,128)S(1)} %copy.8.labels_ref, f32[8,512]{1,0:T(8,128)S(1)} %get-tuple-element.13.keep_ref, ...), custom_call_target="tpu_custom_call" | custom-call | tf_op jit(solution)/shard_map/pallas_call | solution.py:274
  58.9 5.6 %all-to-all-start.2 = ((bf16[8,112,512]{2,1,0:T(8,128)(2,1)}), bf16[8,112,512]{2,1,0:T(8,128)(2,1)S(1)}, u32[]{:S(2)}, u32[]{:S(2)}) async-start(bf16[8,112,512]{2,1,0:T(8,128)(2,1)} %shard_map.66), calls=%async_computation.2 | async-start | bytes 1835008 | tf_op jit(solution)/shard_map/all_to_all | solution.py:244
  64.5 0.0 copy-done.1
  64.5 1.9 %collective-permute-start.1 = (bf16[1,501,501]{2,1,0:T(8,128)(2,1)S(1)}, bf16[1,501,501]{2,1,0:T(8,128)(2,1)S(1)}, u32[]{:S(2)}, u32[]{:S(2)}) collective-permute-start(bf16[1,501,501]{2,1,0:T(8,128)(2,1)S(1)} %copy-done.1), channel_id=1, source_target_pairs={{0,8},{8,0},{1,9},{9,1},{2,10},{10,2},{3,11},{11,3},{4,12},{12,4},... | collective-permute-start | bytes 1506014 | tf_op jit(solution)/shard_map/ppermute | solution.py:248
  66.5 0.0 copy-done.2
  66.5 0.1 convert_reduce_fusion.starts_ref
  66.6 1.7 %collective-permute-done.1.other_ref = bf16[1,501,501]{2,1,0:T(8,128)(2,1)S(1)} collective-permute-done((bf16[1,501,501]{2,1,0:T(8,128)(2,1)S(1)}, bf16[1,501,501]{2,1,0:T(8,128)(2,1)S(1)}, u32[]{:S(2)}, u32[]{:S(2)}) %collective-permute-start.1) | collective-permute-done | bytes 502034 | tf_op jit(solution)/shard_map/ppermute | solution.py:248
  68.3 7.7 %all-to-all-done.2.packed_ref = bf16[8,112,512]{2,1,0:T(8,128)(2,1)S(1)} async-done(((bf16[8,112,512]{2,1,0:T(8,128)(2,1)}), bf16[8,112,512]{2,1,0:T(8,128)(2,1)S(1)}, u32[]{:S(2)}, u32[]{:S(2)}) %all-to-all-start.2) | async-done | bytes 917536 | tf_op jit(solution)/shard_map/all_to_all | solution.py:244
  76.0 1.5 %shard_map.67 = (bf16[4,96,512]{2,1,0:T(8,128)(2,1)S(1)}, bf16[8,96,512]{2,1,0:T(8,128)(2,1)}) custom-call(s32[1]{0:T(128)} %bitcast.core_ref, bf16[8,112,512]{2,1,0:T(8,128)(2,1)S(1)} %all-to-all-done.2.packed_ref, bf16[1,501,501]{2,1,0:T(8,128)(2,1)S(1)} %copy-done.1, bf16[1,501,501]{2,1,0:T(8,128)(2,1)S(1)} %collective-permute-done.1.other_ref, ...), custom_call_target="tpu_custom_call" | custom-call | tf_op jit(solution)/shard_map/pallas_call | solution.py:279
  77.6 16.5 %all_to_all.25.pieces_ref = bf16[4,96,512]{2,1,0:T(8,128)(2,1)S(1)} all-to-all(bf16[4,96,512]{2,1,0:T(8,128)(2,1)S(1)} %get-tuple-element.15), channel_id=1, replica_groups=mesh['vocab'=8,'chip'=4,'core'=2,'width'=8] {'chip'}, dimensions={0} | all-to-all | bytes 786432 | tf_op jit(solution)/shard_map/all_to_all | solution.py:244
  94.0 3.5 %all-to-all-start.4 = ((bf16[8,96,512]{2,1,0:T(8,128)(2,1)}), bf16[8,96,512]{2,1,0:T(8,128)(2,1)S(1)}, u32[]{:S(2)}, u32[]{:S(2)}) async-start(bf16[8,96,512]{2,1,0:T(8,128)(2,1)} %get-tuple-element.16), calls=%async_computation.4 | async-start | bytes 1572864 | tf_op jit(solution)/shard_map/all_to_all | solution.py:244
  97.6 0.1 shard_map.68
  97.7 16.5 %all_gather.3.turned_ref = bf16[768,512]{1,0:T(8,128)(2,1)S(1)} all-gather(bf16[96,512]{1,0:T(8,128)(2,1)S(1)} %shard_map.68), channel_id=1, replica_groups=mesh['vocab'=8,'chip'=4,'core'=2,'width'=8] {'chip','core'}, dimensions={0}, use_global_device_ids=true | all-gather | bytes 884736 | tf_op jit(solution)/shard_map/all_gather | solution.py:286
  114.1 6.7 %all-to-all-done.4 = bf16[8,96,512]{2,1,0:T(8,128)(2,1)S(1)} async-done(((bf16[8,96,512]{2,1,0:T(8,128)(2,1)}), bf16[8,96,512]{2,1,0:T(8,128)(2,1)S(1)}, u32[]{:S(2)}, u32[]{:S(2)}) %all-to-all-start.4) | async-done | bytes 786464 | tf_op jit(solution)/shard_map/all_to_all | solution.py:244
  120.9 3.7 %shard_map.69 = f32[501,1,512]{2,1,0:T(1,128)} custom-call(s32[13]{0:T(128)S(1)} %convert_reduce_fusion.starts_ref, bf16[768,512]{1,0:T(8,128)(2,1)S(1)} %all_gather.3.turned_ref, bf16[768,512]{1,0:T(8,128)(2,1)S(1)} %bitcast.7), custom_call_target="tpu_custom_call" | custom-call | tf_op jit(solution)/shard_map/pallas_call | solution.py:225
Async XLA Ops:
  0.0 45.0 %copy-start = (s32[768]{0:T(1024)S(1)}, s32[768]{0:T(1024)}, u32[]{:S(2)}) copy-start(s32[768]{0:T(1024)} %param.10) | copy-start | bytes 9220
  5.4 23.1 %all-to-all-start = ((s16[16,64,512]{2,1,0:T(8,128)(2,1)}), s16[16,64,512]{2,1,0:T(8,128)(2,1)S(1)}, u32[]{:S(2)}, u32[]{:S(2)}) async-start(s16[16,64,512]{2,1,0:T(8,128)(2,1)} %shard_map.64), calls=%async_computation | async-start | bytes 2097152 | tf_op jit(solution)/shard_map/all_to_all | solution.py:244
  30.6 33.9 %copy-start.1 = (bf16[1,501,501]{2,1,0:T(8,128)(2,1)S(1)}, bf16[1,501,501]{2,1,0:T(8,128)(2,1)}, u32[]{:S(2)}) copy-start(bf16[1,501,501]{2,1,0:T(8,128)(2,1)} %basis_ref.1) | copy-start | bytes 1506010
  30.6 35.8 %copy-start.2 = (s32[768]{0:T(1024)S(1)}, s32[768]{0:T(1024)}, u32[]{:S(2)}) copy-start(s32[768]{0:T(1024)} %param.11) | copy-start | bytes 9220
  30.6 14.6 %collective-permute-start = (f32[8,512]{1,0:T(8,128)S(1)}, f32[8,512]{1,0:T(8,128)S(1)}, u32[]{:S(2)}, u32[]{:S(2)}) collective-permute-start(f32[8,512]{1,0:T(8,128)S(1)} %get-tuple-element.14), channel_id=1, source_target_pairs={{0,8},{8,0},{1,9},{9,1},{2,10},{10,2},{3,11},{11,3},{4,12},{12,4},... | collective-permute-start | bytes 49160 | tf_op jit(solution)/shard_map/ppermute | solution.py:248
  32.7 24.5 %all-to-all-start.1 = ((f32[32,2,128]{2,1,0:T(2,128)}), f32[32,2,128]{2,1,0:T(2,128)S(1)}, u32[]{:S(2)}, u32[]{:S(2)}) async-start(f32[32,2,128]{2,1,0:T(2,128)} %get-tuple-element.12), calls=%async_computation.1 | async-start | bytes 65536 | tf_op jit(solution)/shard_map/all_to_all | solution.py:244
  58.9 17.1 %all-to-all-start.2 = ((bf16[8,112,512]{2,1,0:T(8,128)(2,1)}), bf16[8,112,512]{2,1,0:T(8,128)(2,1)S(1)}, u32[]{:S(2)}, u32[]{:S(2)}) async-start(bf16[8,112,512]{2,1,0:T(8,128)(2,1)} %shard_map.66), calls=%async_computation.2 | async-start | bytes 1835008 | tf_op jit(solution)/shard_map/all_to_all | solution.py:244
  64.5 3.8 %collective-permute-start.1 = (bf16[1,501,501]{2,1,0:T(8,128)(2,1)S(1)}, bf16[1,501,501]{2,1,0:T(8,128)(2,1)S(1)}, u32[]{:S(2)}, u32[]{:S(2)}) collective-permute-start(bf16[1,501,501]{2,1,0:T(8,128)(2,1)S(1)} %copy-done.1), channel_id=1, source_target_pairs={{0,8},{8,0},{1,9},{9,1},{2,10},{10,2},{3,11},{11,3},{4,12},{12,4},... | collective-permute-start | bytes 1506014 | tf_op jit(solution)/shard_map/ppermute | solution.py:248
  94.0 26.8 %all-to-all-start.4 = ((bf16[8,96,512]{2,1,0:T(8,128)(2,1)}), bf16[8,96,512]{2,1,0:T(8,128)(2,1)S(1)}, u32[]{:S(2)}, u32[]{:S(2)}) async-start(bf16[8,96,512]{2,1,0:T(8,128)(2,1)} %get-tuple-element.16), calls=%async_computation.4 | async-start | bytes 1572864 | tf_op jit(solution)/shard_map/all_to_all | solution.py:244

commit v4 on v2

--- a/solution.py
+++ b/solution.py
@@ -19,6 +19,7 @@
 DEALT = BLOCK // PARTS
 SHARE = 8
 ROWS = BLOCK + SHARE
+PAIRS = BLOCK // 2
 LANES = 512
 WINDOW = SEQ_LEN + 16
 VMEM = 48 * 1024 * 1024
@@ -50,6 +51,25 @@
     return (width // CORES * CORES + core) * GROUP + width % CORES * BLOCK
 
 
+def step_of(exponent):
+    return jnp.exp2(exponent)
+
+
+def encode(values, bits):
+    top, low = jnp.max(values, axis=1, keepdims=True), jnp.min(values, axis=1, keepdims=True)
+    middle, radius = 0.5 * top + 0.5 * low, 0.5 * top - 0.5 * low
+    least = jnp.maximum(radius / (0.97 * 2.0 ** (bits - 1)), jnp.abs(middle) * 2.0**-29)
+    exponent = jnp.ceil(jnp.log2(jnp.maximum(least, 2.0**-100)))
+    step = step_of(exponent)
+    offset = jnp.floor(middle / step + 0.5)
+    high = jnp.floor(offset / 32768.0)
+    return jnp.floor((values - offset * step) / step + 0.5), (exponent, high, offset - high * 32768.0)
+
+
+def whole(values):
+    return values.astype(jnp.int32).astype(jnp.int16)
+
+
 def partial_kernel(place_ref, hidden_ref, mine_ref, unembed_ref, width_ref, out_ref):
     rows = unembed_ref.shape[1]
     logits = lax.dot_general(
@@ -62,18 +82,32 @@
 
     dealt = jnp.dot(pick((CORES * PARTS * SHARE, GROUP), source), mine_ref[...], preferred_element_type=jnp.float32)
     projected = jnp.dot(dealt.astype(jnp.bfloat16), width_ref[...], preferred_element_type=jnp.float32)
+    projected, share_notes = encode(projected, 16)
+    logits, logit_notes = encode(logits, 24)
+    high = jnp.floor(logits / 256.0 + 0.5)
+    low = logits - high * 256.0
+    lane = lax.broadcasted_iota(jnp.int32, (BLOCK, LANES - rows), 1)
+    rest = jnp.zeros((BLOCK - SHARE, 1), jnp.float32)
     for core in range(CORES):
         for width in range(PARTS):
             owner, begin = core * PARTS + width, owned(core, width)
-            out_ref[owner, :BLOCK, rows:] = jnp.zeros((BLOCK, LANES - rows), jnp.float32)
-            out_ref[owner, :BLOCK, :rows] = logits[begin : begin + BLOCK]
-            out_ref[owner, BLOCK:, :] = projected[owner * SHARE : (owner + 1) * SHARE]
+            tokens, shares = slice(begin, begin + BLOCK), slice(owner * SHARE, (owner + 1) * SHARE)
+            notes = jnp.zeros((BLOCK, LANES - rows), jnp.float32)
+            for number, part in enumerate(logit_notes):
+                notes = jnp.where(lane == number, part[tokens], notes)
+            for number, part in enumerate(share_notes):
+                notes = jnp.where(lane == 3 + number, jnp.concatenate([part[shares], rest], axis=0), notes)
+            out_ref[owner, :BLOCK, :rows] = whole(high[tokens])
+            out_ref[owner, :BLOCK, rows:] = whole(notes)
+            pairs = low[begin : begin + PAIRS] * 256.0 + (low[begin + PAIRS : begin + BLOCK] + 128.0)
+            pairs = jnp.concatenate([pairs, jnp.zeros((PAIRS, LANES - rows), jnp.float32)], axis=1)
+            out_ref[owner, BLOCK:, :] = whole(jnp.concatenate([pairs, projected[shares]], axis=0))
 
 
 def partial_sums(place, hidden, unembed, rotate_width):
     return pl.pallas_call(
         partial_kernel,
-        out_shape=jax.ShapeDtypeStruct((CORES * PARTS, ROWS, LANES), jnp.float32),
+        out_shape=jax.ShapeDtypeStruct((CORES * PARTS, ROWS + PAIRS, LANES), jnp.int16),
         grid_spec=pltpu.PrefetchScalarGridSpec(
             num_scalar_prefetch=1,
             grid=(1,),
@@ -83,14 +117,31 @@
                 pl.BlockSpec(unembed.shape, lambda g, place: (0, 0, 0)),
                 pl.BlockSpec(rotate_width.shape, lambda g, place: (0, 0)),
             ],
-            out_specs=pl.BlockSpec((CORES * PARTS, ROWS, LANES), lambda g, place: (0, 0, 0)),
+            out_specs=pl.BlockSpec((CORES * PARTS, ROWS + PAIRS, LANES), lambda g, place: (0, 0, 0)),
         ),
         compiler_params=pltpu.CompilerParams(vmem_limit_bytes=MOST),
     )(place, hidden, hidden, unembed, rotate_width)
 
 
+def decode(rows, pieces_ref, owner):
+    high = pieces_ref[owner, :BLOCK].astype(jnp.int32).astype(jnp.float32)
+    rest = pieces_ref[owner, BLOCK:].astype(jnp.int32).astype(jnp.float32)
+    notes, pairs, share = high[:, rows:], rest[:PAIRS], rest[PAIRS:]
+    first = jnp.floor(pairs / 256.0)
+    low = jnp.concatenate([first, pairs - first * 256.0 - 128.0], axis=0)
+
+    def offset(notes):
+        return notes[:, 0:1] * 32768.0 + notes[:, 1:2]
+
+    step = step_of(notes[:, 0:1])
+    logits = (high * 256.0 + low) * step + offset(notes[:, 1:3]) * step
+    step = step_of(notes[:SHARE, 3:4])
+    share = share * step + offset(notes[:SHARE, 4:6]) * step
+    return jnp.concatenate([logits, share], axis=0)
+
+
 def local_kernel(rows, core_ref, pieces_ref, logits_ref, stats_ref, keep_ref, send_ref):
-    sums = [jnp.sum(pieces_ref[core * PARTS : (core + 1) * PARTS], axis=0) for core in range(CORES)]
+    sums = [sum(decode(rows, pieces_ref, core * PARTS + width) for width in range(PARTS)) for core in range(CORES)]
     column = lax.broadcasted_iota(jnp.int32, (CORES * BLOCK, LANES), 1)
     logits = jnp.concatenate([part[:BLOCK] for part in sums], axis=0)
     logits = jnp.where(column < rows, logits, -jnp.inf)

time: 129 us -> 126 us (0.977)
  the two profiles are of different devices: /device:TPU:67 before, /device:TPU:66 now
where the time goes in v4:
time: 126 us; the launch traced here: 125 us
  waiting for transfers between devices  43.8 us (35%)
  starting transfers between devices  33.5 us (27%)
  blocking collectives  32.8 us (26%)
  Pallas kernels  14.9 us (12%)
    all_to_all x4, waiting for transfers between devices, exchange(): return lax.all_to_all(values, axis, 0, 0, tiled=True)  41.1 us
    all_to_all x4, starting transfers between devices, exchange(): return lax.all_to_all(values, axis, 0, 0, tiled=True)  29.7 us
    all_to_all x1, blocking collectives, exchange(): return lax.all_to_all(values, axis, 0, 0, tiled=True)  16.5 us
    all_gather x1, blocking collectives, body(): turned = lax.all_gather(turned, ROW, axis=0, tiled=True)  16.3 us
    pallas_call x1, Pallas kernels, partial_sums(): pl.pallas_call(partial_kernel, out_shape=jax.ShapeDtypeStruct((CORES * PA...  5.53 us
    ppermute x2, starting transfers between devices, swap(): lax.ppermute(values, 'core', [(i, CORES - 1 - i) for i in range(CORES)])  3.83 us
    pallas_call x1, Pallas kernels, gradients(): pl.pallas_call(gradient_kernel, out_shape=jax.ShapeDtypeStruct((height, 1...  3.73 us
    ppermute x2, waiting for transfers between devices, swap(): lax.ppermute(values, 'core', [(i, CORES - 1 - i) for i in range(CORES)])  2.7 us
  transfers between devices with their start and end apart: 6, of which 6 were waited for; matrix products, arithmetic and copies ran while one was open for 0% of the time, Pallas kernels for 0%

profile of v4, /device:TPU:66, one launch (start us, length us, event | category | flops | bytes accessed | tf_op | source)
XLA Modules:
  0.0 125.4 jit_solution(6724360110564071703)
XLA Ops:
  0.0 0.0 copy-start
  0.0 5.5 %shard_map.64 = s16[16,80,512]{2,1,0:T(8,128)(2,1)} custom-call(s32[1]{0:T(128)} %bitcast.2.place_ref, bf16[768,1024]{1,0:T(8,128)(2,1)} %mine_ref.1, bf16[768,1024]{1,0:T(8,128)(2,1)} %mine_ref.1, bf16[1,501,1024]{2,1,0:T(8,128)(2,1)} %unembed_ref.1, bf16[1024,512]{1,0:T(8,128)(2,1)} %width_ref.1), custom_call_target="tpu_custom_call" | custom-call | tf_op jit(solution)/shard_map/pallas_call | solution.py:108
  5.5 8.5 %all-to-all-start = ((s16[16,80,512]{2,1,0:T(8,128)(2,1)}), s16[16,80,512]{2,1,0:T(8,128)(2,1)S(1)}, u32[]{:S(2)}, u32[]{:S(2)}) async-start(s16[16,80,512]{2,1,0:T(8,128)(2,1)} %shard_map.64), calls=%async_computation | async-start | bytes 2621440 | tf_op jit(solution)/shard_map/all_to_all | solution.py:251
  14.1 0.1 pad_add_fusion.place_ref
  14.1 17.3 %all-to-all-done.pieces_ref = s16[16,80,512]{2,1,0:T(8,128)(2,1)S(1)} async-done(((s16[16,80,512]{2,1,0:T(8,128)(2,1)}), s16[16,80,512]{2,1,0:T(8,128)(2,1)S(1)}, u32[]{:S(2)}, u32[]{:S(2)}) %all-to-all-start) | async-done | bytes 1310752 | tf_op jit(solution)/shard_map/all_to_all | solution.py:251
  31.5 2.3 %shard_map.65 = (f32[96,512]{1,0:T(8,128)S(1)}, f32[32,2,128]{2,1,0:T(2,128)}, f32[8,512]{1,0:T(8,128)S(1)}, f32[8,512]{1,0:T(8,128)S(1)}) custom-call(s32[1]{0:T(128)} %bitcast.core_ref, s16[16,80,512]{2,1,0:T(8,128)(2,1)S(1)} %all-to-all-done.pieces_ref), custom_call_target="tpu_custom_call" | custom-call | tf_op jit(solution)/shard_map/pallas_call | solution.py:270
  33.8 12.2 %all-to-all-start.1 = ((f32[32,2,128]{2,1,0:T(2,128)}), f32[32,2,128]{2,1,0:T(2,128)S(1)}, u32[]{:S(2)}, u32[]{:S(2)}) async-start(f32[32,2,128]{2,1,0:T(2,128)} %get-tuple-element.12), calls=%async_computation.1 | async-start | bytes 65536 | tf_op jit(solution)/shard_map/all_to_all | solution.py:251
  46.0 1.9 %collective-permute-start = (f32[8,512]{1,0:T(8,128)S(1)}, f32[8,512]{1,0:T(8,128)S(1)}, u32[]{:S(2)}, u32[]{:S(2)}) collective-permute-start(f32[8,512]{1,0:T(8,128)S(1)} %get-tuple-element.14), channel_id=1, source_target_pairs={{0,8},{8,0},{1,9},{9,1},{2,10},{10,2},{3,11},{11,3},{4,12},{12,4},... | collective-permute-start | bytes 49160 | tf_op jit(solution)/shard_map/ppermute | solution.py:255
  47.9 0.0 copy-done
  47.9 0.1 dynamic-slice_bitcast_fusion
  48.0 0.1 copy.8.labels_ref
  48.1 1.0 collective-permute-done.got_ref
  49.1 9.2 %all-to-all-done.1.stats_ref = f32[32,2,128]{2,1,0:T(2,128)S(1)} async-done(((f32[32,2,128]{2,1,0:T(2,128)}), f32[32,2,128]{2,1,0:T(2,128)S(1)}, u32[]{:S(2)}, u32[]{:S(2)}) %all-to-all-start.1) | async-done | bytes 32800 | tf_op jit(solution)/shard_map/all_to_all | solution.py:251
  58.3 0.0 copy-start.1
  58.3 0.0 copy-start.2
  58.3 1.7 %shard_map.66 = bf16[8,112,512]{2,1,0:T(8,128)(2,1)} custom-call(s32[2]{0:T(128)S(1)} %pad_add_fusion.place_ref, f32[96,512]{1,0:T(8,128)S(1)} %get-tuple-element.11.logits_ref, f32[32,2,128]{2,1,0:T(2,128)S(1)} %all-to-all-done.1.stats_ref, s32[48,1]{1,0:T(8,128)S(1)} %copy.8.labels_ref, f32[8,512]{1,0:T(8,128)S(1)} %get-tuple-element.13.keep_ref, ...), custom_call_target="tpu_custom_call" | custom-call | tf_op jit(solution)/shard_map/pallas_call | solution.py:281
  60.0 5.4 %all-to-all-start.2 = ((bf16[8,112,512]{2,1,0:T(8,128)(2,1)}), bf16[8,112,512]{2,1,0:T(8,128)(2,1)S(1)}, u32[]{:S(2)}, u32[]{:S(2)}) async-start(bf16[8,112,512]{2,1,0:T(8,128)(2,1)} %shard_map.66), calls=%async_computation.2 | async-start | bytes 1835008 | tf_op jit(solution)/shard_map/all_to_all | solution.py:251
  65.3 0.0 copy-done.1
  65.3 1.9 %collective-permute-start.1 = (bf16[1,501,501]{2,1,0:T(8,128)(2,1)S(1)}, bf16[1,501,501]{2,1,0:T(8,128)(2,1)S(1)}, u32[]{:S(2)}, u32[]{:S(2)}) collective-permute-start(bf16[1,501,501]{2,1,0:T(8,128)(2,1)S(1)} %copy-done.1), channel_id=1, source_target_pairs={{0,8},{8,0},{1,9},{9,1},{2,10},{10,2},{3,11},{11,3},{4,12},{12,4},... | collective-permute-start | bytes 1506014 | tf_op jit(solution)/shard_map/ppermute | solution.py:255
  67.3 0.0 copy-done.2
  67.3 0.1 convert_reduce_fusion.starts_ref
  67.4 1.7 %collective-permute-done.1.other_ref = bf16[1,501,501]{2,1,0:T(8,128)(2,1)S(1)} collective-permute-done((bf16[1,501,501]{2,1,0:T(8,128)(2,1)S(1)}, bf16[1,501,501]{2,1,0:T(8,128)(2,1)S(1)}, u32[]{:S(2)}, u32[]{:S(2)}) %collective-permute-start.1) | collective-permute-done | bytes 502034 | tf_op jit(solution)/shard_map/ppermute | solution.py:255
  69.1 7.7 %all-to-all-done.2.packed_ref = bf16[8,112,512]{2,1,0:T(8,128)(2,1)S(1)} async-done(((bf16[8,112,512]{2,1,0:T(8,128)(2,1)}), bf16[8,112,512]{2,1,0:T(8,128)(2,1)S(1)}, u32[]{:S(2)}, u32[]{:S(2)}) %all-to-all-start.2) | async-done | bytes 917536 | tf_op jit(solution)/shard_map/all_to_all | solution.py:251
  76.8 1.5 %shard_map.67 = (bf16[4,96,512]{2,1,0:T(8,128)(2,1)S(1)}, bf16[8,96,512]{2,1,0:T(8,128)(2,1)}) custom-call(s32[1]{0:T(128)} %bitcast.core_ref, bf16[8,112,512]{2,1,0:T(8,128)(2,1)S(1)} %all-to-all-done.2.packed_ref, bf16[1,501,501]{2,1,0:T(8,128)(2,1)S(1)} %copy-done.1, bf16[1,501,501]{2,1,0:T(8,128)(2,1)S(1)} %collective-permute-done.1.other_ref, ...), custom_call_target="tpu_custom_call" | custom-call | tf_op jit(solution)/shard_map/pallas_call | solution.py:286
  78.4 16.5 %all_to_all.25.pieces_ref = bf16[4,96,512]{2,1,0:T(8,128)(2,1)S(1)} all-to-all(bf16[4,96,512]{2,1,0:T(8,128)(2,1)S(1)} %get-tuple-element.15), channel_id=1, replica_groups=mesh['vocab'=8,'chip'=4,'core'=2,'width'=8] {'chip'}, dimensions={0} | all-to-all | bytes 786432 | tf_op jit(solution)/shard_map/all_to_all | solution.py:251
  94.9 3.5 %all-to-all-start.4 = ((bf16[8,96,512]{2,1,0:T(8,128)(2,1)}), bf16[8,96,512]{2,1,0:T(8,128)(2,1)S(1)}, u32[]{:S(2)}, u32[]{:S(2)}) async-start(bf16[8,96,512]{2,1,0:T(8,128)(2,1)} %get-tuple-element.16), calls=%async_computation.4 | async-start | bytes 1572864 | tf_op jit(solution)/shard_map/all_to_all | solution.py:251
  98.4 0.1 shard_map.68
  98.5 16.3 %all_gather.3.turned_ref = bf16[768,512]{1,0:T(8,128)(2,1)S(1)} all-gather(bf16[96,512]{1,0:T(8,128)(2,1)S(1)} %shard_map.68), channel_id=1, replica_groups=mesh['vocab'=8,'chip'=4,'core'=2,'width'=8] {'chip','core'}, dimensions={0}, use_global_device_ids=true | all-gather | bytes 884736 | tf_op jit(solution)/shard_map/all_gather | solution.py:293
  114.8 6.9 %all-to-all-done.4 = bf16[8,96,512]{2,1,0:T(8,128)(2,1)S(1)} async-done(((bf16[8,96,512]{2,1,0:T(8,128)(2,1)}), bf16[8,96,512]{2,1,0:T(8,128)(2,1)S(1)}, u32[]{:S(2)}, u32[]{:S(2)}) %all-to-all-start.4) | async-done | bytes 786464 | tf_op jit(solution)/shard_map/all_to_all | solution.py:251
  121.7 3.7 %shard_map.69 = f32[501,1,512]{2,1,0:T(1,128)} custom-call(s32[13]{0:T(128)S(1)} %convert_reduce_fusion.starts_ref, bf16[768,512]{1,0:T(8,128)(2,1)S(1)} %all_gather.3.turned_ref, bf16[768,512]{1,0:T(8,128)(2,1)S(1)} %bitcast.7), custom_call_target="tpu_custom_call" | custom-call | tf_op jit(solution)/shard_map/pallas_call | solution.py:232
Async XLA Ops:
  0.0 47.9 %copy-start = (s32[768]{0:T(1024)S(1)}, s32[768]{0:T(1024)}, u32[]{:S(2)}) copy-start(s32[768]{0:T(1024)} %param.10) | copy-start | bytes 9220
  5.5 25.9 %all-to-all-start = ((s16[16,80,512]{2,1,0:T(8,128)(2,1)}), s16[16,80,512]{2,1,0:T(8,128)(2,1)S(1)}, u32[]{:S(2)}, u32[]{:S(2)}) async-start(s16[16,80,512]{2,1,0:T(8,128)(2,1)} %shard_map.64), calls=%async_computation | async-start | bytes 2621440 | tf_op jit(solution)/shard_map/all_to_all | solution.py:251
  33.8 24.5 %all-to-all-start.1 = ((f32[32,2,128]{2,1,0:T(2,128)}), f32[32,2,128]{2,1,0:T(2,128)S(1)}, u32[]{:S(2)}, u32[]{:S(2)}) async-start(f32[32,2,128]{2,1,0:T(2,128)} %get-tuple-element.12), calls=%async_computation.1 | async-start | bytes 65536 | tf_op jit(solution)/shard_map/all_to_all | solution.py:251
  46.0 3.1 %collective-permute-start = (f32[8,512]{1,0:T(8,128)S(1)}, f32[8,512]{1,0:T(8,128)S(1)}, u32[]{:S(2)}, u32[]{:S(2)}) collective-permute-start(f32[8,512]{1,0:T(8,128)S(1)} %get-tuple-element.14), channel_id=1, source_target_pairs={{0,8},{8,0},{1,9},{9,1},{2,10},{10,2},{3,11},{11,3},{4,12},{12,4},... | collective-permute-start | bytes 49160 | tf_op jit(solution)/shard_map/ppermute | solution.py:255
  58.3 7.1 %copy-start.1 = (bf16[1,501,501]{2,1,0:T(8,128)(2,1)S(1)}, bf16[1,501,501]{2,1,0:T(8,128)(2,1)}, u32[]{:S(2)}) copy-start(bf16[1,501,501]{2,1,0:T(8,128)(2,1)} %basis_ref.1) | copy-start | bytes 1506010
  58.3 9.0 %copy-start.2 = (s32[768]{0:T(1024)S(1)}, s32[768]{0:T(1024)}, u32[]{:S(2)}) copy-start(s32[768]{0:T(1024)} %param.11) | copy-start | bytes 9220
  60.0 16.9 %all-to-all-start.2 = ((bf16[8,112,512]{2,1,0:T(8,128)(2,1)}), bf16[8,112,512]{2,1,0:T(8,128)(2,1)S(1)}, u32[]{:S(2)}, u32[]{:S(2)}) async-start(bf16[8,112,512]{2,1,0:T(8,128)(2,1)} %shard_map.66), calls=%async_computation.2 | async-start | bytes 1835008 | tf_op jit(solution)/shard_map/all_to_all | solution.py:251
  65.3 3.8 %collective-permute-start.1 = (bf16[1,501,501]{2,1,0:T(8,128)(2,1)S(1)}, bf16[1,501,501]{2,1,0:T(8,128)(2,1)S(1)}, u32[]{:S(2)}, u32[]{:S(2)}) collective-permute-start(bf16[1,501,501]{2,1,0:T(8,128)(2,1)S(1)} %copy-done.1), channel_id=1, source_target_pairs={{0,8},{8,0},{1,9},{9,1},{2,10},{10,2},{3,11},{11,3},{4,12},{12,4},... | collective-permute-start | bytes 1506014 | tf_op jit(solution)/shard_map/ppermute | solution.py:255
  94.9 26.8 %all-to-all-start.4 = ((bf16[8,96,512]{2,1,0:T(8,128)(2,1)}), bf16[8,96,512]{2,1,0:T(8,128)(2,1)S(1)}, u32[]{:S(2)}, u32[]{:S(2)}) async-start(bf16[8,96,512]{2,1,0:T(8,128)(2,1)} %get-tuple-element.16), calls=%async_computation.4 | async-start | bytes 1572864 | tf_op jit(solution)/shard_map/all_to_all | solution.py:251

commit v5 on v4

--- a/solution.py
+++ b/solution.py
@@ -140,15 +140,13 @@
     return jnp.concatenate([logits, share], axis=0)
 
 
-def local_kernel(rows, core_ref, pieces_ref, logits_ref, stats_ref, keep_ref, send_ref):
+def local_kernel(rows, pieces_ref, logits_ref, stats_ref, share_ref):
     sums = [sum(decode(rows, pieces_ref, core * PARTS + width) for width in range(PARTS)) for core in range(CORES)]
     column = lax.broadcasted_iota(jnp.int32, (CORES * BLOCK, LANES), 1)
     logits = jnp.concatenate([part[:BLOCK] for part in sums], axis=0)
     logits = jnp.where(column < rows, logits, -jnp.inf)
     logits_ref[...] = logits
-    first = core_ref[0] == 0
-    keep_ref[...] = jnp.where(first, sums[0][BLOCK:], sums[1][BLOCK:])
-    send_ref[...] = jnp.where(first, sums[1][BLOCK:], sums[0][BLOCK:])
+    share_ref[...] = jnp.concatenate([part[BLOCK:] for part in sums], axis=0).astype(jnp.bfloat16)
     largest = jnp.max(logits, axis=1, keepdims=True)
     largest = jnp.maximum(largest[:BLOCK], largest[BLOCK:])
     total = jnp.sum(jnp.exp(logits - jnp.concatenate([largest, largest], axis=0)), axis=1, keepdims=True)
@@ -162,7 +160,13 @@
         stats_ref[device] = tile
 
 
-def error_kernel(rows, place_ref, logits_ref, stats_ref, labels_ref, keep_ref, got_ref, out_ref):
+def merge_kernel(stats_ref, out_ref):
+    largest = jnp.max(stats_ref[:, 0:1, :], axis=0)
+    total = jnp.sum(stats_ref[:, 1:2, :] * jnp.exp(stats_ref[:, 0:1, :] - largest[None]), axis=0)
+    out_ref[0] = jnp.concatenate([largest, total], axis=0)
+
+
+def error_kernel(rows, first_ref, logits_ref, stats_ref, labels_ref, share_ref, out_ref):
     largest = jnp.max(stats_ref[:, 0:1, :], axis=0)
     total = jnp.sum(stats_ref[:, 1:2, :] * jnp.exp(stats_ref[:, 0:1, :] - largest[None]), axis=0)
     row = lax.broadcasted_iota(jnp.int32, (128, 128), 0)
@@ -172,18 +176,15 @@
     parts = []
     for core in range(CORES):
         probabilities = jnp.exp(logits_ref[core * BLOCK : (core + 1) * BLOCK] - largest) / total
-        hit = (labels_ref[...] - (place_ref[1] + core * rows) == column) & (column < rows)
+        hit = (labels_ref[...] - (first_ref[0] + core * rows) == column) & (column < rows)
         parts.append((probabilities - hit.astype(jnp.float32)).astype(jnp.bfloat16))
     errors = jnp.concatenate(parts, axis=0)
-    first = place_ref[0] == 0
-    keep, got = keep_ref[...], got_ref[...]
-    share = jnp.concatenate([jnp.where(first, keep, got), jnp.where(first, got, keep)], axis=0).astype(jnp.bfloat16)
     for piece in range(PARTS):
         out_ref[piece, : CORES * BLOCK] = errors
-        out_ref[piece, CORES * BLOCK :] = share
-
-
-def turn_kernel(core_ref, packed_ref, basis_ref, other_ref, starts_ref, out_ref, share_ref):
+        out_ref[piece, CORES * BLOCK :] = share_ref[...]
+
+
+def turn_kernel(core_ref, packed_ref, basis_ref, other_ref, starts_ref, out_ref, keep_ref, send_ref):
     rows = basis_ref.shape[1]
     turned = 0.0
     for core, ref in ((core_ref[0], basis_ref), (1 - core_ref[0], other_ref)):
@@ -193,11 +194,28 @@
         )
     out_ref[:, :, :rows] = turned.astype(jnp.bfloat16).reshape(CHIPS, GROUP, rows)
     out_ref[:, :, rows:] = jnp.zeros((CHIPS, GROUP, LANES - rows), jnp.bfloat16)
-    dealt = packed_ref[:, CORES * BLOCK :, :].reshape(PARTS * CORES * SHARE, LANES)
-    order = pick((GROUP, PARTS * CORES * SHARE), lambda row: row // DEALT * SHARE + lax.rem(row, DEALT))
-    share = jnp.dot(order, dealt, preferred_element_type=jnp.float32).astype(jnp.bfloat16)
+    share = packed_ref[:, GROUP:, :].astype(jnp.float32)
+    first, second = share[:, :SHARE], share[:, SHARE:]
+    first_core = core_ref[0] == 0
+    keep, send = jnp.where(first_core, first, second), jnp.where(first_core, second, first)
+    keep_ref[...] = keep.reshape(PARTS * SHARE, LANES).astype(jnp.bfloat16)
+    send_ref[...] = send.reshape(PARTS * SHARE, LANES).astype(jnp.bfloat16)
+
+
+def share_kernel(core_ref, keep_ref, got_ref, out_ref):
+    def order(core):
+        def source(row):
+            owner, within = row // DEALT, lax.rem(row, DEALT)
+            return jnp.where(lax.rem(owner, CORES) == core, owner // CORES * SHARE + within, -1)
+
+        return pick((GROUP, PARTS * SHARE), source)
+
+    core = core_ref[0]
+    share = jnp.dot(order(core), keep_ref[...], preferred_element_type=jnp.float32)
+    share += jnp.dot(order(1 - core), got_ref[...], preferred_element_type=jnp.float32)
+    share = share.astype(jnp.bfloat16)
     for piece in range(PARTS):
-        share_ref[piece] = share
+        out_ref[piece] = share
 
 
 def sum_kernel(pieces_ref, out_ref):
@@ -258,7 +276,7 @@
 def body(hidden, unembed, rotate_vocab, rotate_width, labels, seq_ids):
     rows = unembed.shape[1]
     vocab, chip, core, width = (lax.axis_index(a).astype(jnp.int32) for a in ("vocab", "chip", "core", "width"))
-    place = jnp.stack([core, (vocab * PARTS + chip * CORES) * rows])
+    first = ((vocab * PARTS + chip * CORES) * rows).reshape(1)
     core = core.reshape(1)
     mine = lax.dynamic_slice_in_dim(labels, owned(core[0], width), BLOCK, 0).reshape(BLOCK, 1)
     sequence_index = jnp.arange(SEQS + 1, dtype=jnp.int32)
@@ -267,27 +285,25 @@
 
     pieces = partial_sums(vocab.reshape(1), hidden, unembed, rotate_width)
     pieces = exchange(pieces, ("core", "width"))
-    logits, stats, keep, send = call(
+    logits, stats, share = call(
         functools.partial(local_kernel, rows),
-        [
-            ((CORES * BLOCK, LANES), single),
-            ((PARTS * CHIPS, 2, 128), single),
-            ((SHARE, LANES), single),
-            ((SHARE, LANES), single),
-        ],
-        [SCALARS, FULL],
-    )(core, pieces)
-    stats = exchange(stats, ("vocab", "chip"))
+        [((GROUP, LANES), single), ((1, 2, 128), single), ((CORES * SHARE, LANES), half)],
+        [FULL],
+    )(pieces)
+    stats = lax.all_gather(stats, "vocab", axis=0, tiled=True)
+    stats = call(merge_kernel, [((1, 2, 128), single)], [FULL])(stats)
+    stats = lax.all_gather(stats, "chip", axis=0, tiled=True)
     packed = call(
         functools.partial(error_kernel, rows),
         [((PARTS, CORES * ROWS, LANES), half)],
-        [SCALARS, FULL, FULL, FULL, FULL, FULL],
-    )(place, logits, stats, mine, keep, swap(send))
-    turned, share = call(
+        [SCALARS, FULL, FULL, FULL, FULL],
+    )(first, logits, stats, mine, share)
+    turned, keep, send = call(
         turn_kernel,
-        [((CHIPS, GROUP, LANES), half), ((PARTS, GROUP, LANES), half)],
+        [((CHIPS, GROUP, LANES), half), ((PARTS * SHARE, LANES), half), ((PARTS * SHARE, LANES), half)],
         [SCALARS, FULL, FULL, FULL, pl.BlockSpec(memory_space=pl.ANY)],
     )(core, exchange(packed, "width"), rotate_vocab, swap(rotate_vocab), starts)
+    share = call(share_kernel, [((PARTS, GROUP, LANES), half)], [SCALARS, FULL, FULL])(core, keep, swap(send))
     projected = exchange(share, "vocab").reshape(TOKENS, LANES)
     turned = call(sum_kernel, [((GROUP, LANES), half)], [FULL])(exchange(turned, "chip"))
     turned = lax.all_gather(turned, ROW, axis=0, tiled=True)

time: 126 us -> 122 us (0.968)
  the two profiles are of different devices: /device:TPU:66 before, /device:TPU:1 now
where the time goes in v5:
time: 122 us
  blocking collectives  47.8 us (39%)
  starting transfers between devices  37.9 us (31%)
  waiting for transfers between devices  21.1 us (17%)
  Pallas kernels  14.6 us (12%)
    all_gather x1, blocking collectives, body(): turned = lax.all_gather(turned, ROW, axis=0, tiled=True)  23.5 us
    all_to_all x4, starting transfers between devices, exchange(): return lax.all_to_all(values, axis, 0, 0, tiled=True)  21.5 us
    all_to_all x4, waiting for transfers between devices, exchange(): return lax.all_to_all(values, axis, 0, 0, tiled=True)  18.8 us
    ppermute x2, starting transfers between devices, swap(): lax.ppermute(values, 'core', [(i, CORES - 1 - i) for i in range(CORES)])  16.4 us
    all_gather x1, blocking collectives, body(): stats = lax.all_gather(stats, 'chip', axis=0, tiled=True)  14.1 us
    all_gather x1, blocking collectives, body(): stats = lax.all_gather(stats, 'vocab', axis=0, tiled=True)  10.2 us
    pallas_call x1, Pallas kernels, partial_sums(): pl.pallas_call(partial_kernel, out_shape=jax.ShapeDtypeStruct((CORES * PA...  5.53 us
    pallas_call x1, Pallas kernels, gradients(): pl.pallas_call(gradient_kernel, out_shape=jax.ShapeDtypeStruct((height, 1...  3.73 us
  transfers between devices with their start and end apart: 6, of which 3 were waited for; matrix products, arithmetic and copies ran while one was open for 0% of the time, Pallas kernels for 1%

profile of v5, /device:TPU:1, one launch (start us, length us, event | category | flops | bytes accessed | tf_op | source)
XLA Modules:
  0.0 121.7 jit_solution(5682813751211608621)
XLA Ops:
  0.0 0.0 copy-start
  0.0 5.5 %shard_map.64 = s16[16,80,512]{2,1,0:T(8,128)(2,1)} custom-call(s32[1]{0:T(128)} %bitcast.2.place_ref, bf16[768,1024]{1,0:T(8,128)(2,1)} %mine_ref.1, bf16[768,1024]{1,0:T(8,128)(2,1)} %mine_ref.1, bf16[1,501,1024]{2,1,0:T(8,128)(2,1)} %unembed_ref.1, bf16[1024,512]{1,0:T(8,128)(2,1)} %width_ref.1), custom_call_target="tpu_custom_call" | custom-call | tf_op jit(solution)/shard_map/pallas_call | solution.py:108
  5.5 10.4 %all-to-all-start = ((s16[16,80,512]{2,1,0:T(8,128)(2,1)}), s16[16,80,512]{2,1,0:T(8,128)(2,1)S(1)}, u32[]{:S(2)}, u32[]{:S(2)}) async-start(s16[16,80,512]{2,1,0:T(8,128)(2,1)} %shard_map.64), calls=%async_computation | async-start | bytes 2621440 | tf_op jit(solution)/shard_map/all_to_all | solution.py:269
  16.0 0.0 copy-done
  16.0 0.1 dynamic-slice_bitcast_fusion
  16.0 0.1 copy.9.labels_ref
  16.1 18.8 %all-to-all-done.pieces_ref = s16[16,80,512]{2,1,0:T(8,128)(2,1)S(1)} async-done(((s16[16,80,512]{2,1,0:T(8,128)(2,1)}), s16[16,80,512]{2,1,0:T(8,128)(2,1)S(1)}, u32[]{:S(2)}, u32[]{:S(2)}) %all-to-all-start) | async-done | bytes 1310752 | tf_op jit(solution)/shard_map/all_to_all | solution.py:269
  34.9 1.7 %shard_map.65 = (f32[96,512]{1,0:T(8,128)S(1)}, f32[1,2,128]{2,1,0:T(2,128)S(1)}, bf16[16,512]{1,0:T(8,128)(2,1)S(1)}) custom-call(s16[16,80,512]{2,1,0:T(8,128)(2,1)S(1)} %all-to-all-done.pieces_ref), custom_call_target="tpu_custom_call" | custom-call | tf_op jit(solution)/shard_map/pallas_call | solution.py:288
  36.6 10.2 %all_gather.9.stats_ref = f32[8,2,128]{2,1,0:T(2,128)S(1)} all-gather(f32[1,2,128]{2,1,0:T(2,128)S(1)} %get-tuple-element.12), channel_id=1, replica_groups=mesh['vocab'=8,'chip'=4,'core'=2,'width'=8] {'vocab'}, dimensions={0}, use_global_device_ids=true | all-gather | bytes 9216 | tf_op jit(solution)/shard_map/all_gather | solution.py:293
  46.8 14.1 %all_gather.10.stats_ref = f32[4,2,128]{2,1,0:T(2,128)S(1)} all-gather(f32[1,2,128]{2,1,0:T(2,128)S(1)} %shard_map.66), channel_id=1, replica_groups=mesh['vocab'=8,'chip'=4,'core'=2,'width'=8] {'chip'}, dimensions={0}, use_global_device_ids=true | all-gather | bytes 5120 | tf_op jit(solution)/shard_map/all_gather | solution.py:295
  61.0 0.0 copy-start.1
  61.0 0.0 copy-start.2
  61.0 1.1 shard_map.67
  62.1 3.6 %all-to-all-start.1 = ((bf16[8,112,512]{2,1,0:T(8,128)(2,1)}), bf16[8,112,512]{2,1,0:T(8,128)(2,1)S(1)}, u32[]{:S(2)}, u32[]{:S(2)}) async-start(bf16[8,112,512]{2,1,0:T(8,128)(2,1)} %shard_map.67), calls=%async_computation.1 | async-start | bytes 1835008 | tf_op jit(solution)/shard_map/all_to_all | solution.py:269
  65.7 0.0 copy-done.1
  65.7 7.8 %collective-permute-start = (bf16[1,501,501]{2,1,0:T(8,128)(2,1)S(1)}, bf16[1,501,501]{2,1,0:T(8,128)(2,1)S(1)}, u32[]{:S(2)}, u32[]{:S(2)}) collective-permute-start(bf16[1,501,501]{2,1,0:T(8,128)(2,1)S(1)} %copy-done.1), channel_id=1, source_target_pairs={{0,8},{8,0},{1,9},{9,1},{2,10},{10,2},{3,11},{11,3},{4,12},{12,4},... | collective-permute-start | bytes 1506014 | tf_op jit(solution)/shard_map/ppermute | solution.py:273
  73.5 0.0 copy-done.2
  73.5 0.1 convert_reduce_fusion.starts_ref
  73.6 1.4 %collective-permute-done.other_ref = bf16[1,501,501]{2,1,0:T(8,128)(2,1)S(1)} collective-permute-done((bf16[1,501,501]{2,1,0:T(8,128)(2,1)S(1)}, bf16[1,501,501]{2,1,0:T(8,128)(2,1)S(1)}, u32[]{:S(2)}, u32[]{:S(2)}) %collective-permute-start) | collective-permute-done | bytes 502034 | tf_op jit(solution)/shard_map/ppermute | solution.py:273
  75.0 0.0 all-to-all-done.1.packed_ref
  75.0 1.3 %shard_map.68 = (bf16[4,96,512]{2,1,0:T(8,128)(2,1)}, bf16[64,512]{1,0:T(8,128)(2,1)S(1)}, bf16[64,512]{1,0:T(8,128)(2,1)S(1)}) custom-call(s32[1]{0:T(128)} %bitcast.core_ref, bf16[8,112,512]{2,1,0:T(8,128)(2,1)S(1)} %all-to-all-done.1.packed_ref, bf16[1,501,501]{2,1,0:T(8,128)(2,1)S(1)} %copy-done.1, ...), custom_call_target="tpu_custom_call" | custom-call | tf_op jit(solution)/shard_map/pallas_call | solution.py:301
  76.3 3.5 %all-to-all-start.2 = ((bf16[4,96,512]{2,1,0:T(8,128)(2,1)}), bf16[4,96,512]{2,1,0:T(8,128)(2,1)S(1)}, u32[]{:S(2)}, u32[]{:S(2)}) async-start(bf16[4,96,512]{2,1,0:T(8,128)(2,1)} %get-tuple-element.14), calls=%async_computation.2 | async-start | bytes 786432 | tf_op jit(solution)/shard_map/all_to_all | solution.py:269
  79.8 8.6 %collective-permute-start.1 = (bf16[64,512]{1,0:T(8,128)(2,1)S(1)}, bf16[64,512]{1,0:T(8,128)(2,1)S(1)}, u32[]{:S(2)}, u32[]{:S(2)}) collective-permute-start(bf16[64,512]{1,0:T(8,128)(2,1)S(1)} %get-tuple-element.16), channel_id=1, source_target_pairs={{0,8},{8,0},{1,9},{9,1},{2,10},{10,2},{3,11},{11,3},{4,12},{12,4},... | collective-permute-start | bytes 196616 | tf_op jit(solution)/shard_map/ppermute | solution.py:273
  88.4 0.9 collective-permute-done.1.got_ref
  89.3 1.1 shard_map.70
  90.4 0.0 all-to-all-done.2.pieces_ref
  90.4 4.0 %all-to-all-start.3 = ((bf16[8,96,512]{2,1,0:T(8,128)(2,1)}), bf16[8,96,512]{2,1,0:T(8,128)(2,1)S(1)}, u32[]{:S(2)}, u32[]{:S(2)}) async-start(bf16[8,96,512]{2,1,0:T(8,128)(2,1)} %shard_map.70), calls=%async_computation.3 | async-start | bytes 1572864 | tf_op jit(solution)/shard_map/all_to_all | solution.py:269
  94.5 0.1 shard_map.69
  94.5 23.5 %all_gather.11.turned_ref = bf16[768,512]{1,0:T(8,128)(2,1)S(1)} all-gather(bf16[96,512]{1,0:T(8,128)(2,1)S(1)} %shard_map.69), channel_id=1, replica_groups=mesh['vocab'=8,'chip'=4,'core'=2,'width'=8] {'chip','core'}, dimensions={0}, use_global_device_ids=true | all-gather | bytes 884736 | tf_op jit(solution)/shard_map/all_gather | solution.py:309
  118.0 0.0 all-to-all-done.3
  118.0 3.7 %shard_map.71 = f32[501,1,512]{2,1,0:T(1,128)} custom-call(s32[13]{0:T(128)S(1)} %convert_reduce_fusion.starts_ref, bf16[768,512]{1,0:T(8,128)(2,1)S(1)} %all_gather.11.turned_ref, bf16[768,512]{1,0:T(8,128)(2,1)S(1)} %bitcast.7), custom_call_target="tpu_custom_call" | custom-call | tf_op jit(solution)/shard_map/pallas_call | solution.py:250
  (1 shorter events, 0.0 us)
Async XLA Ops:
  0.0 16.0 %copy-start = (s32[768]{0:T(1024)S(1)}, s32[768]{0:T(1024)}, u32[]{:S(2)}) copy-start(s32[768]{0:T(1024)} %param.10) | copy-start | bytes 9220
  5.5 29.4 %all-to-all-start = ((s16[16,80,512]{2,1,0:T(8,128)(2,1)}), s16[16,80,512]{2,1,0:T(8,128)(2,1)S(1)}, u32[]{:S(2)}, u32[]{:S(2)}) async-start(s16[16,80,512]{2,1,0:T(8,128)(2,1)} %shard_map.64), calls=%async_computation | async-start | bytes 2621440 | tf_op jit(solution)/shard_map/all_to_all | solution.py:269
  61.0 4.7 %copy-start.1 = (bf16[1,501,501]{2,1,0:T(8,128)(2,1)S(1)}, bf16[1,501,501]{2,1,0:T(8,128)(2,1)}, u32[]{:S(2)}) copy-start(bf16[1,501,501]{2,1,0:T(8,128)(2,1)} %basis_ref.1) | copy-start | bytes 1506010
  61.0 12.5 %copy-start.2 = (s32[768]{0:T(1024)S(1)}, s32[768]{0:T(1024)}, u32[]{:S(2)}) copy-start(s32[768]{0:T(1024)} %param.11) | copy-start | bytes 9220
  62.1 12.8 %all-to-all-start.1 = ((bf16[8,112,512]{2,1,0:T(8,128)(2,1)}), bf16[8,112,512]{2,1,0:T(8,128)(2,1)S(1)}, u32[]{:S(2)}, u32[]{:S(2)}) async-start(bf16[8,112,512]{2,1,0:T(8,128)(2,1)} %shard_map.67), calls=%async_computation.1 | async-start | bytes 1835008 | tf_op jit(solution)/shard_map/all_to_all | solution.py:269
  65.7 9.3 %collective-permute-start = (bf16[1,501,501]{2,1,0:T(8,128)(2,1)S(1)}, bf16[1,501,501]{2,1,0:T(8,128)(2,1)S(1)}, u32[]{:S(2)}, u32[]{:S(2)}) collective-permute-start(bf16[1,501,501]{2,1,0:T(8,128)(2,1)S(1)} %copy-done.1), channel_id=1, source_target_pairs={{0,8},{8,0},{1,9},{9,1},{2,10},{10,2},{3,11},{11,3},{4,12},{12,4},... | collective-permute-start | bytes 1506014 | tf_op jit(solution)/shard_map/ppermute | solution.py:273
  76.3 14.1 %all-to-all-start.2 = ((bf16[4,96,512]{2,1,0:T(8,128)(2,1)}), bf16[4,96,512]{2,1,0:T(8,128)(2,1)S(1)}, u32[]{:S(2)}, u32[]{:S(2)}) async-start(bf16[4,96,512]{2,1,0:T(8,128)(2,1)} %get-tuple-element.14), calls=%async_computation.2 | async-start | bytes 786432 | tf_op jit(solution)/shard_map/all_to_all | solution.py:269
  79.8 9.5 %collective-permute-start.1 = (bf16[64,512]{1,0:T(8,128)(2,1)S(1)}, bf16[64,512]{1,0:T(8,128)(2,1)S(1)}, u32[]{:S(2)}, u32[]{:S(2)}) collective-permute-start(bf16[64,512]{1,0:T(8,128)(2,1)S(1)} %get-tuple-element.16), channel_id=1, source_target_pairs={{0,8},{8,0},{1,9},{9,1},{2,10},{10,2},{3,11},{11,3},{4,12},{12,4},... | collective-permute-start | bytes 196616 | tf_op jit(solution)/shard_map/ppermute | solution.py:273
  90.4 27.6 %all-to-all-start.3 = ((bf16[8,96,512]{2,1,0:T(8,128)(2,1)}), bf16[8,96,512]{2,1,0:T(8,128)(2,1)S(1)}, u32[]{:S(2)}, u32[]{:S(2)}) async-start(bf16[8,96,512]{2,1,0:T(8,128)(2,1)} %shard_map.70), calls=%async_computation.3 | async-start | bytes 1572864 | tf_op jit(solution)/shard_map/all_to_all | solution.py:269

commit v6 on v5

--- a/solution.py
+++ b/solution.py
@@ -21,6 +21,7 @@
 ROWS = BLOCK + SHARE
 PAIRS = BLOCK // 2
 LANES = 512
+CHUNKS = 2
 WINDOW = SEQ_LEN + 16
 VMEM = 48 * 1024 * 1024
 MOST = 60 * 1024 * 1024
@@ -70,17 +71,34 @@
     return values.astype(jnp.int32).astype(jnp.int16)
 
 
-def partial_kernel(place_ref, hidden_ref, mine_ref, unembed_ref, width_ref, out_ref):
+def partial_kernel(
+    place_ref, hidden_hbm, unembed_hbm, width_hbm, out_ref, hidden_ref, unembed_ref, width_ref, logits_ref, sems
+):
     rows = unembed_ref.shape[1]
-    logits = lax.dot_general(
-        hidden_ref[...], unembed_ref[0], (((1,), (1,)), ((), ())), preferred_element_type=jnp.float32
-    )
+    chunk = TOKENS // CHUNKS
+    copies = [pltpu.make_async_copy(unembed_hbm, unembed_ref, sems.at[CHUNKS])]
+    for number in range(CHUNKS):
+        part = pl.ds(number * chunk, chunk)
+        copies.append(pltpu.make_async_copy(hidden_hbm.at[part], hidden_ref.at[part], sems.at[number]))
+    copies.append(pltpu.make_async_copy(width_hbm, width_ref, sems.at[CHUNKS + 1]))
+    for copy in copies:
+        copy.start()
+    copies[0].wait()
+    for number in range(CHUNKS):
+        copies[1 + number].wait()
+        part = slice(number * chunk, (number + 1) * chunk)
+        logits_ref[part] = lax.dot_general(
+            hidden_ref[part], unembed_ref[0], (((1,), (1,)), ((), ())), preferred_element_type=jnp.float32
+        )
+    copies[-1].wait()
+    logits = logits_ref[...]
+    mine = hidden_ref[pl.ds(pl.multiple_of(place_ref[0] * GROUP, GROUP), GROUP), :]
 
     def source(row):
         core, width, within = row // (PARTS * SHARE), lax.rem(row // SHARE, PARTS), lax.rem(row, SHARE)
         return jnp.where(within < DEALT, (width * CORES + core) * DEALT + within, -1)
 
-    dealt = jnp.dot(pick((CORES * PARTS * SHARE, GROUP), source), mine_ref[...], preferred_element_type=jnp.float32)
+    dealt = jnp.dot(pick((CORES * PARTS * SHARE, GROUP), source), mine, preferred_element_type=jnp.float32)
     projected = jnp.dot(dealt.astype(jnp.bfloat16), width_ref[...], preferred_element_type=jnp.float32)
     projected, share_notes = encode(projected, 16)
     logits, logit_notes = encode(logits, 24)
@@ -105,22 +123,21 @@
 
 
 def partial_sums(place, hidden, unembed, rotate_width):
+    anywhere = pl.BlockSpec(memory_space=pl.ANY)
     return pl.pallas_call(
         partial_kernel,
         out_shape=jax.ShapeDtypeStruct((CORES * PARTS, ROWS + PAIRS, LANES), jnp.int16),
-        grid_spec=pltpu.PrefetchScalarGridSpec(
-            num_scalar_prefetch=1,
-            grid=(1,),
-            in_specs=[
-                pl.BlockSpec(hidden.shape, lambda g, place: (0, 0)),
-                pl.BlockSpec((GROUP, hidden.shape[1]), lambda g, place: (place[0], 0)),
-                pl.BlockSpec(unembed.shape, lambda g, place: (0, 0, 0)),
-                pl.BlockSpec(rotate_width.shape, lambda g, place: (0, 0)),
-            ],
-            out_specs=pl.BlockSpec((CORES * PARTS, ROWS + PAIRS, LANES), lambda g, place: (0, 0, 0)),
-        ),
+        in_specs=[SCALARS, anywhere, anywhere, anywhere],
+        out_specs=FULL,
+        scratch_shapes=[
+            pltpu.VMEM(hidden.shape, hidden.dtype),
+            pltpu.VMEM(unembed.shape, unembed.dtype),
+            pltpu.VMEM(rotate_width.shape, rotate_width.dtype),
+            pltpu.VMEM((TOKENS, unembed.shape[1]), jnp.float32),
+            pltpu.SemaphoreType.DMA((CHUNKS + 2,)),
+        ],
         compiler_params=pltpu.CompilerParams(vmem_limit_bytes=MOST),
-    )(place, hidden, hidden, unembed, rotate_width)
+    )(place, hidden, unembed, rotate_width)
 
 
 def decode(rows, pieces_ref, owner):
@@ -140,7 +157,7 @@
     return jnp.concatenate([logits, share], axis=0)
 
 
-def local_kernel(rows, pieces_ref, logits_ref, stats_ref, share_ref):
+def local_kernel(rows, pieces_ref, unread_ref, logits_ref, stats_ref, share_ref):
     sums = [sum(decode(rows, pieces_ref, core * PARTS + width) for width in range(PARTS)) for core in range(CORES)]
     column = lax.broadcasted_iota(jnp.int32, (CORES * BLOCK, LANES), 1)
     logits = jnp.concatenate([part[:BLOCK] for part in sums], axis=0)
@@ -246,7 +263,7 @@
 
 def gradients(starts, turned, projected, height):
     width = projected.shape[1]
-    tile = 256
+    tile = 512
     out = pl.pallas_call(
         gradient_kernel,
         out_shape=jax.ShapeDtypeStruct((height, 1, width), jnp.float32),
@@ -285,11 +302,12 @@
 
     pieces = partial_sums(vocab.reshape(1), hidden, unembed, rotate_width)
     pieces = exchange(pieces, ("core", "width"))
+    other = swap(rotate_vocab)
     logits, stats, share = call(
         functools.partial(local_kernel, rows),
         [((GROUP, LANES), single), ((1, 2, 128), single), ((CORES * SHARE, LANES), half)],
-        [FULL],
-    )(pieces)
+        [FULL, pl.BlockSpec(memory_space=pl.ANY)],
+    )(pieces, other)
     stats = lax.all_gather(stats, "vocab", axis=0, tiled=True)
     stats = call(merge_kernel, [((1, 2, 128), single)], [FULL])(stats)
     stats = lax.all_gather(stats, "chip", axis=0, tiled=True)
@@ -302,7 +320,7 @@
         turn_kernel,
         [((CHIPS, GROUP, LANES), half), ((PARTS * SHARE, LANES), half), ((PARTS * SHARE, LANES), half)],
         [SCALARS, FULL, FULL, FULL, pl.BlockSpec(memory_space=pl.ANY)],
-    )(core, exchange(packed, "width"), rotate_vocab, swap(rotate_vocab), starts)
+    )(core, exchange(packed, "width"), rotate_vocab, other, starts)
     share = call(share_kernel, [((PARTS, GROUP, LANES), half)], [SCALARS, FULL, FULL])(core, keep, swap(send))
     projected = exchange(share, "vocab").reshape(TOKENS, LANES)
     turned = call(sum_kernel, [((GROUP, LANES), half)], [FULL])(exchange(turned, "chip"))

time: 122 us -> 122 us (level)
  starting transfers between devices: 37.9 us -> 32.8 us
  waiting for transfers between devices: 21.1 us -> 26.2 us
    ppermute x2, starting transfers between devices: 16.4 us -> 11.2 us  [swap(): lax.ppermute(values, 'core', [(i, CORES - 1 - i) for i in range(CORES)])]
    all_to_all x4, waiting for transfers between devices: 18.8 us -> 23.8 us  [exchange(): return lax.all_to_all(values, axis, 0, 0, tiled=True)]
  transfers between devices with their start and end apart: 6 -> 6, of which waited for: 3 -> 4; matrix products, arithmetic and copies ran while one was open for 0% -> 0% of each run, Pallas kernels for 1% -> 1%
where the time goes in v6:
time: 122 us
  blocking collectives  47.8 us (39%)
  starting transfers between devices  32.8 us (27%)
  waiting for transfers between devices  26.2 us (21%)
  Pallas kernels  14.3 us (12%)
    all_to_all x4, waiting for transfers between devices, exchange(): return lax.all_to_all(values, axis, 0, 0, tiled=True)  23.8 us
    all_gather x1, blocking collectives, body(): turned = lax.all_gather(turned, ROW, axis=0, tiled=True)  23.5 us
    all_to_all x4, starting transfers between devices, exchange(): return lax.all_to_all(values, axis, 0, 0, tiled=True)  21.6 us
    all_gather x1, blocking collectives, body(): stats = lax.all_gather(stats, 'chip', axis=0, tiled=True)  14.1 us
    ppermute x2, starting transfers between devices, swap(): lax.ppermute(values, 'core', [(i, CORES - 1 - i) for i in range(CORES)])  11.2 us
    all_gather x1, blocking collectives, body(): stats = lax.all_gather(stats, 'vocab', axis=0, tiled=True)  10.2 us
    pallas_call x1, Pallas kernels, partial_sums(): pl.pallas_call(partial_kernel, out_shape=jax.ShapeDtypeStruct((CORES * PA...  5.31 us
    pallas_call x1, Pallas kernels, gradients(): pl.pallas_call(gradient_kernel, out_shape=jax.ShapeDtypeStruct((height, 1...  3.58 us
  transfers between devices with their start and end apart: 6, of which 4 were waited for; matrix products, arithmetic and copies ran while one was open for 0% of the time, Pallas kernels for 1%

profile of v6, /device:TPU:1, one launch (start us, length us, event | category | flops | bytes accessed | tf_op | source)
XLA Modules:
  0.0 121.6 jit_solution(8877660146694387770)
XLA Ops:
  0.0 0.0 copy-start
  0.0 5.3 %shard_map.64 = s16[16,80,512]{2,1,0:T(8,128)(2,1)} custom-call(s32[1]{0:T(128)} %bitcast.2.place_ref, bf16[768,1024]{1,0:T(8,128)(2,1)} %hidden_hbm.1, bf16[1,501,1024]{2,1,0:T(8,128)(2,1)} %unembed_hbm.1, bf16[1024,512]{1,0:T(8,128)(2,1)} %width_hbm.1), custom_call_target="tpu_custom_call" | custom-call | tf_op jit(solution)/shard_map/pallas_call | solution.py:127
  5.3 0.0 copy-start.1
  5.3 10.6 %all-to-all-start = ((s16[16,80,512]{2,1,0:T(8,128)(2,1)}), s16[16,80,512]{2,1,0:T(8,128)(2,1)S(1)}, u32[]{:S(2)}, u32[]{:S(2)}) async-start(s16[16,80,512]{2,1,0:T(8,128)(2,1)} %shard_map.64), calls=%async_computation | async-start | bytes 2621440 | tf_op jit(solution)/shard_map/all_to_all | solution.py:286
  15.9 0.0 copy-done.1
  15.9 2.1 %collective-permute-start = (bf16[1,501,501]{2,1,0:T(8,128)(2,1)S(1)}, bf16[1,501,501]{2,1,0:T(8,128)(2,1)S(1)}, u32[]{:S(2)}, u32[]{:S(2)}) collective-permute-start(bf16[1,501,501]{2,1,0:T(8,128)(2,1)S(1)} %copy-done.1), channel_id=1, source_target_pairs={{0,8},{8,0},{1,9},{9,1},{2,10},{10,2},{3,11},{11,3},{4,12},{12,4},... | collective-permute-start | bytes 1506014 | tf_op jit(solution)/shard_map/ppermute | solution.py:290
  18.0 0.0 copy-done
  18.0 0.1 dynamic-slice_bitcast_fusion
  18.1 0.1 copy.9.labels_ref
  18.2 1.5 %collective-permute-done.unread_ref.other_ref = bf16[1,501,501]{2,1,0:T(8,128)(2,1)S(1)} collective-permute-done((bf16[1,501,501]{2,1,0:T(8,128)(2,1)S(1)}, bf16[1,501,501]{2,1,0:T(8,128)(2,1)S(1)}, u32[]{:S(2)}, u32[]{:S(2)}) %collective-permute-start) | collective-permute-done | bytes 502034 | tf_op jit(solution)/shard_map/ppermute | solution.py:290
  19.7 15.2 %all-to-all-done.pieces_ref = s16[16,80,512]{2,1,0:T(8,128)(2,1)S(1)} async-done(((s16[16,80,512]{2,1,0:T(8,128)(2,1)}), s16[16,80,512]{2,1,0:T(8,128)(2,1)S(1)}, u32[]{:S(2)}, u32[]{:S(2)}) %all-to-all-start) | async-done | bytes 1310752 | tf_op jit(solution)/shard_map/all_to_all | solution.py:286
  34.9 1.7 %shard_map.65 = (f32[96,512]{1,0:T(8,128)S(1)}, f32[1,2,128]{2,1,0:T(2,128)S(1)}, bf16[16,512]{1,0:T(8,128)(2,1)S(1)}) custom-call(s16[16,80,512]{2,1,0:T(8,128)(2,1)S(1)} %all-to-all-done.pieces_ref, bf16[1,501,501]{2,1,0:T(8,128)(2,1)S(1)} %collective-permute-done.unread_ref.other_ref), custom_call_target="tpu_custom_call" | custom-call | tf_op jit(solution)/shard_map/pallas_call | solution.py:306
  36.6 10.2 %all_gather.9.stats_ref = f32[8,2,128]{2,1,0:T(2,128)S(1)} all-gather(f32[1,2,128]{2,1,0:T(2,128)S(1)} %get-tuple-element.12), channel_id=1, replica_groups=mesh['vocab'=8,'chip'=4,'core'=2,'width'=8] {'vocab'}, dimensions={0}, use_global_device_ids=true | all-gather | bytes 9216 | tf_op jit(solution)/shard_map/all_gather | solution.py:311
  46.8 14.1 %all_gather.10.stats_ref = f32[4,2,128]{2,1,0:T(2,128)S(1)} all-gather(f32[1,2,128]{2,1,0:T(2,128)S(1)} %shard_map.66), channel_id=1, replica_groups=mesh['vocab'=8,'chip'=4,'core'=2,'width'=8] {'chip'}, dimensions={0}, use_global_device_ids=true | all-gather | bytes 5120 | tf_op jit(solution)/shard_map/all_gather | solution.py:313
  60.9 0.0 copy-start.2
  60.9 1.1 shard_map.67
  62.0 3.6 %all-to-all-start.1 = ((bf16[8,112,512]{2,1,0:T(8,128)(2,1)}), bf16[8,112,512]{2,1,0:T(8,128)(2,1)S(1)}, u32[]{:S(2)}, u32[]{:S(2)}) async-start(bf16[8,112,512]{2,1,0:T(8,128)(2,1)} %shard_map.67), calls=%async_computation.1 | async-start | bytes 1835008 | tf_op jit(solution)/shard_map/all_to_all | solution.py:286
  65.6 0.0 copy-done.2
  65.6 0.1 convert_reduce_fusion.starts_ref
  65.7 8.7 %all-to-all-done.1.packed_ref = bf16[8,112,512]{2,1,0:T(8,128)(2,1)S(1)} async-done(((bf16[8,112,512]{2,1,0:T(8,128)(2,1)}), bf16[8,112,512]{2,1,0:T(8,128)(2,1)S(1)}, u32[]{:S(2)}, u32[]{:S(2)}) %all-to-all-start.1) | async-done | bytes 917536 | tf_op jit(solution)/shard_map/all_to_all | solution.py:286
  74.4 1.4 %shard_map.68 = (bf16[4,96,512]{2,1,0:T(8,128)(2,1)}, bf16[64,512]{1,0:T(8,128)(2,1)S(1)}, bf16[64,512]{1,0:T(8,128)(2,1)S(1)}) custom-call(s32[1]{0:T(128)} %bitcast.core_ref, bf16[8,112,512]{2,1,0:T(8,128)(2,1)S(1)} %all-to-all-done.1.packed_ref, bf16[1,501,501]{2,1,0:T(8,128)(2,1)S(1)} %copy-done.1, ...), custom_call_target="tpu_custom_call" | custom-call | tf_op jit(solution)/shard_map/pallas_call | solution.py:319
  75.7 3.5 %all-to-all-start.2 = ((bf16[4,96,512]{2,1,0:T(8,128)(2,1)}), bf16[4,96,512]{2,1,0:T(8,128)(2,1)S(1)}, u32[]{:S(2)}, u32[]{:S(2)}) async-start(bf16[4,96,512]{2,1,0:T(8,128)(2,1)} %get-tuple-element.14), calls=%async_computation.2 | async-start | bytes 786432 | tf_op jit(solution)/shard_map/all_to_all | solution.py:286
  79.2 9.1 %collective-permute-start.1 = (bf16[64,512]{1,0:T(8,128)(2,1)S(1)}, bf16[64,512]{1,0:T(8,128)(2,1)S(1)}, u32[]{:S(2)}, u32[]{:S(2)}) collective-permute-start(bf16[64,512]{1,0:T(8,128)(2,1)S(1)} %get-tuple-element.16), channel_id=1, source_target_pairs={{0,8},{8,0},{1,9},{9,1},{2,10},{10,2},{3,11},{11,3},{4,12},{12,4},... | collective-permute-start | bytes 196616 | tf_op jit(solution)/shard_map/ppermute | solution.py:290
  88.4 0.9 collective-permute-done.1.got_ref
  89.2 1.1 shard_map.70
  90.4 0.0 all-to-all-done.2.pieces_ref
  90.4 4.0 %all-to-all-start.3 = ((bf16[8,96,512]{2,1,0:T(8,128)(2,1)}), bf16[8,96,512]{2,1,0:T(8,128)(2,1)S(1)}, u32[]{:S(2)}, u32[]{:S(2)}) async-start(bf16[8,96,512]{2,1,0:T(8,128)(2,1)} %shard_map.70), calls=%async_computation.3 | async-start | bytes 1572864 | tf_op jit(solution)/shard_map/all_to_all | solution.py:286
  94.4 0.1 shard_map.69
  94.5 23.5 %all_gather.11.turned_ref = bf16[768,512]{1,0:T(8,128)(2,1)S(1)} all-gather(bf16[96,512]{1,0:T(8,128)(2,1)S(1)} %shard_map.69), channel_id=1, replica_groups=mesh['vocab'=8,'chip'=4,'core'=2,'width'=8] {'chip','core'}, dimensions={0}, use_global_device_ids=true | all-gather | bytes 884736 | tf_op jit(solution)/shard_map/all_gather | solution.py:327
  118.0 0.0 all-to-all-done.3
  118.0 3.6 %shard_map.71 = f32[501,1,512]{2,1,0:T(1,128)} custom-call(s32[13]{0:T(128)S(1)} %convert_reduce_fusion.starts_ref, bf16[768,512]{1,0:T(8,128)(2,1)S(1)} %all_gather.11.turned_ref, bf16[768,512]{1,0:T(8,128)(2,1)S(1)} %bitcast.7), custom_call_target="tpu_custom_call" | custom-call | tf_op jit(solution)/shard_map/pallas_call | solution.py:267
  (1 shorter events, 0.0 us)
Async XLA Ops:
  0.0 18.0 %copy-start = (s32[768]{0:T(1024)S(1)}, s32[768]{0:T(1024)}, u32[]{:S(2)}) copy-start(s32[768]{0:T(1024)} %param.10) | copy-start | bytes 9220
  5.3 10.6 %copy-start.1 = (bf16[1,501,501]{2,1,0:T(8,128)(2,1)S(1)}, bf16[1,501,501]{2,1,0:T(8,128)(2,1)}, u32[]{:S(2)}) copy-start(bf16[1,501,501]{2,1,0:T(8,128)(2,1)} %basis_ref.1) | copy-start | bytes 1506010
  5.3 29.5 %all-to-all-start = ((s16[16,80,512]{2,1,0:T(8,128)(2,1)}), s16[16,80,512]{2,1,0:T(8,128)(2,1)S(1)}, u32[]{:S(2)}, u32[]{:S(2)}) async-start(s16[16,80,512]{2,1,0:T(8,128)(2,1)} %shard_map.64), calls=%async_computation | async-start | bytes 2621440 | tf_op jit(solution)/shard_map/all_to_all | solution.py:286
  15.9 3.8 %collective-permute-start = (bf16[1,501,501]{2,1,0:T(8,128)(2,1)S(1)}, bf16[1,501,501]{2,1,0:T(8,128)(2,1)S(1)}, u32[]{:S(2)}, u32[]{:S(2)}) collective-permute-start(bf16[1,501,501]{2,1,0:T(8,128)(2,1)S(1)} %copy-done.1), channel_id=1, source_target_pairs={{0,8},{8,0},{1,9},{9,1},{2,10},{10,2},{3,11},{11,3},{4,12},{12,4},... | collective-permute-start | bytes 1506014 | tf_op jit(solution)/shard_map/ppermute | solution.py:290
  60.9 4.7 %copy-start.2 = (s32[768]{0:T(1024)S(1)}, s32[768]{0:T(1024)}, u32[]{:S(2)}) copy-start(s32[768]{0:T(1024)} %param.11) | copy-start | bytes 9220
  62.0 12.3 %all-to-all-start.1 = ((bf16[8,112,512]{2,1,0:T(8,128)(2,1)}), bf16[8,112,512]{2,1,0:T(8,128)(2,1)S(1)}, u32[]{:S(2)}, u32[]{:S(2)}) async-start(bf16[8,112,512]{2,1,0:T(8,128)(2,1)} %shard_map.67), calls=%async_computation.1 | async-start | bytes 1835008 | tf_op jit(solution)/shard_map/all_to_all | solution.py:286
  75.7 14.6 %all-to-all-start.2 = ((bf16[4,96,512]{2,1,0:T(8,128)(2,1)}), bf16[4,96,512]{2,1,0:T(8,128)(2,1)S(1)}, u32[]{:S(2)}, u32[]{:S(2)}) async-start(bf16[4,96,512]{2,1,0:T(8,128)(2,1)} %get-tuple-element.14), calls=%async_computation.2 | async-start | bytes 786432 | tf_op jit(solution)/shard_map/all_to_all | solution.py:286
  79.2 10.0 %collective-permute-start.1 = (bf16[64,512]{1,0:T(8,128)(2,1)S(1)}, bf16[64,512]{1,0:T(8,128)(2,1)S(1)}, u32[]{:S(2)}, u32[]{:S(2)}) collective-permute-start(bf16[64,512]{1,0:T(8,128)(2,1)S(1)} %get-tuple-element.16), channel_id=1, source_target_pairs={{0,8},{8,0},{1,9},{9,1},{2,10},{10,2},{3,11},{11,3},{4,12},{12,4},... | collective-permute-start | bytes 196616 | tf_op jit(solution)/shard_map/ppermute | solution.py:290
  90.4 27.6 %all-to-all-start.3 = ((bf16[8,96,512]{2,1,0:T(8,128)(2,1)}), bf16[8,96,512]{2,1,0:T(8,128)(2,1)S(1)}, u32[]{:S(2)}, u32[]{:S(2)}) async-start(bf16[8,96,512]{2,1,0:T(8,128)(2,1)} %shard_map.70), calls=%async_computation.3 | async-start | bytes 1572864 | tf_op jit(solution)/shard_map/all_to_all | solution.py:286

commit v7 on v6

--- a/solution.py
+++ b/solution.py
@@ -21,7 +21,7 @@
 ROWS = BLOCK + SHARE
 PAIRS = BLOCK // 2
 LANES = 512
-CHUNKS = 2
+CHUNKS = 4
 WINDOW = SEQ_LEN + 16
 VMEM = 48 * 1024 * 1024
 MOST = 60 * 1024 * 1024

time: 122 us -> 123 us (level)
  no operation moved by 1% of the time
where the time goes in v7:
time: 123 us; the launch traced here: 122 us
  blocking collectives  47.8 us (39%)
  starting transfers between devices  32.8 us (27%)
  waiting for transfers between devices  26.2 us (21%)
  Pallas kernels  15 us (12%)
    all_to_all x4, waiting for transfers between devices, exchange(): return lax.all_to_all(values, axis, 0, 0, tiled=True)  23.8 us
    all_gather x1, blocking collectives, body(): turned = lax.all_gather(turned, ROW, axis=0, tiled=True)  23.5 us
    all_to_all x4, starting transfers between devices, exchange(): return lax.all_to_all(values, axis, 0, 0, tiled=True)  21.6 us
    all_gather x1, blocking collectives, body(): stats = lax.all_gather(stats, 'chip', axis=0, tiled=True)  14.1 us
    ppermute x2, starting transfers between devices, swap(): lax.ppermute(values, 'core', [(i, CORES - 1 - i) for i in range(CORES)])  11.2 us
    all_gather x1, blocking collectives, body(): stats = lax.all_gather(stats, 'vocab', axis=0, tiled=True)  10.2 us
    pallas_call x1, Pallas kernels, partial_sums(): pl.pallas_call(partial_kernel, out_shape=jax.ShapeDtypeStruct((CORES * PA...  5.99 us
    pallas_call x1, Pallas kernels, gradients(): pl.pallas_call(gradient_kernel, out_shape=jax.ShapeDtypeStruct((height, 1...  3.59 us
  transfers between devices with their start and end apart: 6, of which 4 were waited for; matrix products, arithmetic and copies ran while one was open for 0% of the time, Pallas kernels for 1%

profile of v7, /device:TPU:1, one launch (start us, length us, event | category | flops | bytes accessed | tf_op | source)
XLA Modules:
  0.0 122.3 jit_solution(14679828867518692090)
XLA Ops:
  0.0 0.0 copy-start
  0.0 6.0 %shard_map.64 = s16[16,80,512]{2,1,0:T(8,128)(2,1)} custom-call(s32[1]{0:T(128)} %bitcast.2.place_ref, bf16[768,1024]{1,0:T(8,128)(2,1)} %hidden_hbm.1, bf16[1,501,1024]{2,1,0:T(8,128)(2,1)} %unembed_hbm.1, bf16[1024,512]{1,0:T(8,128)(2,1)} %width_hbm.1), custom_call_target="tpu_custom_call" | custom-call | tf_op jit(solution)/shard_map/pallas_call | solution.py:127
  6.0 0.0 copy-start.1
  6.0 10.6 %all-to-all-start = ((s16[16,80,512]{2,1,0:T(8,128)(2,1)}), s16[16,80,512]{2,1,0:T(8,128)(2,1)S(1)}, u32[]{:S(2)}, u32[]{:S(2)}) async-start(s16[16,80,512]{2,1,0:T(8,128)(2,1)} %shard_map.64), calls=%async_computation | async-start | bytes 2621440 | tf_op jit(solution)/shard_map/all_to_all | solution.py:286
  16.6 0.0 copy-done.1
  16.6 2.1 %collective-permute-start = (bf16[1,501,501]{2,1,0:T(8,128)(2,1)S(1)}, bf16[1,501,501]{2,1,0:T(8,128)(2,1)S(1)}, u32[]{:S(2)}, u32[]{:S(2)}) collective-permute-start(bf16[1,501,501]{2,1,0:T(8,128)(2,1)S(1)} %copy-done.1), channel_id=1, source_target_pairs={{0,8},{8,0},{1,9},{9,1},{2,10},{10,2},{3,11},{11,3},{4,12},{12,4},... | collective-permute-start | bytes 1506014 | tf_op jit(solution)/shard_map/ppermute | solution.py:290
  18.7 0.0 copy-done
  18.7 0.1 dynamic-slice_bitcast_fusion
  18.8 0.1 copy.9.labels_ref
  18.9 1.5 %collective-permute-done.unread_ref.other_ref = bf16[1,501,501]{2,1,0:T(8,128)(2,1)S(1)} collective-permute-done((bf16[1,501,501]{2,1,0:T(8,128)(2,1)S(1)}, bf16[1,501,501]{2,1,0:T(8,128)(2,1)S(1)}, u32[]{:S(2)}, u32[]{:S(2)}) %collective-permute-start) | collective-permute-done | bytes 502034 | tf_op jit(solution)/shard_map/ppermute | solution.py:290
  20.4 15.2 %all-to-all-done.pieces_ref = s16[16,80,512]{2,1,0:T(8,128)(2,1)S(1)} async-done(((s16[16,80,512]{2,1,0:T(8,128)(2,1)}), s16[16,80,512]{2,1,0:T(8,128)(2,1)S(1)}, u32[]{:S(2)}, u32[]{:S(2)}) %all-to-all-start) | async-done | bytes 1310752 | tf_op jit(solution)/shard_map/all_to_all | solution.py:286
  35.6 1.7 %shard_map.65 = (f32[96,512]{1,0:T(8,128)S(1)}, f32[1,2,128]{2,1,0:T(2,128)S(1)}, bf16[16,512]{1,0:T(8,128)(2,1)S(1)}) custom-call(s16[16,80,512]{2,1,0:T(8,128)(2,1)S(1)} %all-to-all-done.pieces_ref, bf16[1,501,501]{2,1,0:T(8,128)(2,1)S(1)} %collective-permute-done.unread_ref.other_ref), custom_call_target="tpu_custom_call" | custom-call | tf_op jit(solution)/shard_map/pallas_call | solution.py:306
  37.2 10.2 %all_gather.9.stats_ref = f32[8,2,128]{2,1,0:T(2,128)S(1)} all-gather(f32[1,2,128]{2,1,0:T(2,128)S(1)} %get-tuple-element.12), channel_id=1, replica_groups=mesh['vocab'=8,'chip'=4,'core'=2,'width'=8] {'vocab'}, dimensions={0}, use_global_device_ids=true | all-gather | bytes 9216 | tf_op jit(solution)/shard_map/all_gather | solution.py:311
  47.5 14.1 %all_gather.10.stats_ref = f32[4,2,128]{2,1,0:T(2,128)S(1)} all-gather(f32[1,2,128]{2,1,0:T(2,128)S(1)} %shard_map.66), channel_id=1, replica_groups=mesh['vocab'=8,'chip'=4,'core'=2,'width'=8] {'chip'}, dimensions={0}, use_global_device_ids=true | all-gather | bytes 5120 | tf_op jit(solution)/shard_map/all_gather | solution.py:313
  61.6 0.0 copy-start.2
  61.6 1.1 shard_map.67
  62.7 3.6 %all-to-all-start.1 = ((bf16[8,112,512]{2,1,0:T(8,128)(2,1)}), bf16[8,112,512]{2,1,0:T(8,128)(2,1)S(1)}, u32[]{:S(2)}, u32[]{:S(2)}) async-start(bf16[8,112,512]{2,1,0:T(8,128)(2,1)} %shard_map.67), calls=%async_computation.1 | async-start | bytes 1835008 | tf_op jit(solution)/shard_map/all_to_all | solution.py:286
  66.3 0.0 copy-done.2
  66.3 0.1 convert_reduce_fusion.starts_ref
  66.4 8.7 %all-to-all-done.1.packed_ref = bf16[8,112,512]{2,1,0:T(8,128)(2,1)S(1)} async-done(((bf16[8,112,512]{2,1,0:T(8,128)(2,1)}), bf16[8,112,512]{2,1,0:T(8,128)(2,1)S(1)}, u32[]{:S(2)}, u32[]{:S(2)}) %all-to-all-start.1) | async-done | bytes 917536 | tf_op jit(solution)/shard_map/all_to_all | solution.py:286
  75.1 1.4 %shard_map.68 = (bf16[4,96,512]{2,1,0:T(8,128)(2,1)}, bf16[64,512]{1,0:T(8,128)(2,1)S(1)}, bf16[64,512]{1,0:T(8,128)(2,1)S(1)}) custom-call(s32[1]{0:T(128)} %bitcast.core_ref, bf16[8,112,512]{2,1,0:T(8,128)(2,1)S(1)} %all-to-all-done.1.packed_ref, bf16[1,501,501]{2,1,0:T(8,128)(2,1)S(1)} %copy-done.1, ...), custom_call_target="tpu_custom_call" | custom-call | tf_op jit(solution)/shard_map/pallas_call | solution.py:319
  76.4 3.5 %all-to-all-start.2 = ((bf16[4,96,512]{2,1,0:T(8,128)(2,1)}), bf16[4,96,512]{2,1,0:T(8,128)(2,1)S(1)}, u32[]{:S(2)}, u32[]{:S(2)}) async-start(bf16[4,96,512]{2,1,0:T(8,128)(2,1)} %get-tuple-element.14), calls=%async_computation.2 | async-start | bytes 786432 | tf_op jit(solution)/shard_map/all_to_all | solution.py:286
  79.9 9.2 %collective-permute-start.1 = (bf16[64,512]{1,0:T(8,128)(2,1)S(1)}, bf16[64,512]{1,0:T(8,128)(2,1)S(1)}, u32[]{:S(2)}, u32[]{:S(2)}) collective-permute-start(bf16[64,512]{1,0:T(8,128)(2,1)S(1)} %get-tuple-element.16), channel_id=1, source_target_pairs={{0,8},{8,0},{1,9},{9,1},{2,10},{10,2},{3,11},{11,3},{4,12},{12,4},... | collective-permute-start | bytes 196616 | tf_op jit(solution)/shard_map/ppermute | solution.py:290
  89.1 0.9 collective-permute-done.1.got_ref
  89.9 1.1 shard_map.70
  91.1 0.0 all-to-all-done.2.pieces_ref
  91.1 4.0 %all-to-all-start.3 = ((bf16[8,96,512]{2,1,0:T(8,128)(2,1)}), bf16[8,96,512]{2,1,0:T(8,128)(2,1)S(1)}, u32[]{:S(2)}, u32[]{:S(2)}) async-start(bf16[8,96,512]{2,1,0:T(8,128)(2,1)} %shard_map.70), calls=%async_computation.3 | async-start | bytes 1572864 | tf_op jit(solution)/shard_map/all_to_all | solution.py:286
  95.1 0.1 shard_map.69
  95.1 23.5 %all_gather.11.turned_ref = bf16[768,512]{1,0:T(8,128)(2,1)S(1)} all-gather(bf16[96,512]{1,0:T(8,128)(2,1)S(1)} %shard_map.69), channel_id=1, replica_groups=mesh['vocab'=8,'chip'=4,'core'=2,'width'=8] {'chip','core'}, dimensions={0}, use_global_device_ids=true | all-gather | bytes 884736 | tf_op jit(solution)/shard_map/all_gather | solution.py:327
  118.7 0.0 all-to-all-done.3
  118.7 3.6 %shard_map.71 = f32[501,1,512]{2,1,0:T(1,128)} custom-call(s32[13]{0:T(128)S(1)} %convert_reduce_fusion.starts_ref, bf16[768,512]{1,0:T(8,128)(2,1)S(1)} %all_gather.11.turned_ref, bf16[768,512]{1,0:T(8,128)(2,1)S(1)} %bitcast.7), custom_call_target="tpu_custom_call" | custom-call | tf_op jit(solution)/shard_map/pallas_call | solution.py:267
  (1 shorter events, 0.0 us)
Async XLA Ops:
  0.0 18.7 %copy-start = (s32[768]{0:T(1024)S(1)}, s32[768]{0:T(1024)}, u32[]{:S(2)}) copy-start(s32[768]{0:T(1024)} %param.10) | copy-start | bytes 9220
  6.0 10.6 %copy-start.1 = (bf16[1,501,501]{2,1,0:T(8,128)(2,1)S(1)}, bf16[1,501,501]{2,1,0:T(8,128)(2,1)}, u32[]{:S(2)}) copy-start(bf16[1,501,501]{2,1,0:T(8,128)(2,1)} %basis_ref.1) | copy-start | bytes 1506010
  6.0 29.6 %all-to-all-start = ((s16[16,80,512]{2,1,0:T(8,128)(2,1)}), s16[16,80,512]{2,1,0:T(8,128)(2,1)S(1)}, u32[]{:S(2)}, u32[]{:S(2)}) async-start(s16[16,80,512]{2,1,0:T(8,128)(2,1)} %shard_map.64), calls=%async_computation | async-start | bytes 2621440 | tf_op jit(solution)/shard_map/all_to_all | solution.py:286
  16.6 3.8 %collective-permute-start = (bf16[1,501,501]{2,1,0:T(8,128)(2,1)S(1)}, bf16[1,501,501]{2,1,0:T(8,128)(2,1)S(1)}, u32[]{:S(2)}, u32[]{:S(2)}) collective-permute-start(bf16[1,501,501]{2,1,0:T(8,128)(2,1)S(1)} %copy-done.1), channel_id=1, source_target_pairs={{0,8},{8,0},{1,9},{9,1},{2,10},{10,2},{3,11},{11,3},{4,12},{12,4},... | collective-permute-start | bytes 1506014 | tf_op jit(solution)/shard_map/ppermute | solution.py:290
  61.6 4.7 %copy-start.2 = (s32[768]{0:T(1024)S(1)}, s32[768]{0:T(1024)}, u32[]{:S(2)}) copy-start(s32[768]{0:T(1024)} %param.11) | copy-start | bytes 9220
  62.7 12.3 %all-to-all-start.1 = ((bf16[8,112,512]{2,1,0:T(8,128)(2,1)}), bf16[8,112,512]{2,1,0:T(8,128)(2,1)S(1)}, u32[]{:S(2)}, u32[]{:S(2)}) async-start(bf16[8,112,512]{2,1,0:T(8,128)(2,1)} %shard_map.67), calls=%async_computation.1 | async-start | bytes 1835008 | tf_op jit(solution)/shard_map/all_to_all | solution.py:286
  76.4 14.6 %all-to-all-start.2 = ((bf16[4,96,512]{2,1,0:T(8,128)(2,1)}), bf16[4,96,512]{2,1,0:T(8,128)(2,1)S(1)}, u32[]{:S(2)}, u32[]{:S(2)}) async-start(bf16[4,96,512]{2,1,0:T(8,128)(2,1)} %get-tuple-element.14), calls=%async_computation.2 | async-start | bytes 786432 | tf_op jit(solution)/shard_map/all_to_all | solution.py:286
  79.9 10.0 %collective-permute-start.1 = (bf16[64,512]{1,0:T(8,128)(2,1)S(1)}, bf16[64,512]{1,0:T(8,128)(2,1)S(1)}, u32[]{:S(2)}, u32[]{:S(2)}) collective-permute-start(bf16[64,512]{1,0:T(8,128)(2,1)S(1)} %get-tuple-element.16), channel_id=1, source_target_pairs={{0,8},{8,0},{1,9},{9,1},{2,10},{10,2},{3,11},{11,3},{4,12},{12,4},... | collective-permute-start | bytes 196616 | tf_op jit(solution)/shard_map/ppermute | solution.py:290
  91.1 27.6 %all-to-all-start.3 = ((bf16[8,96,512]{2,1,0:T(8,128)(2,1)}), bf16[8,96,512]{2,1,0:T(8,128)(2,1)S(1)}, u32[]{:S(2)}, u32[]{:S(2)}) async-start(bf16[8,96,512]{2,1,0:T(8,128)(2,1)} %shard_map.70), calls=%async_computation.3 | async-start | bytes 1572864 | tf_op jit(solution)/shard_map/all_to_all | solution.py:286
